TPU v7x, 128 devices: a whole 4x4x4 slice. The times are simulated.
128 devices in a mesh: dp: 4 (over y), pipe: 4 (over z), expert: 8 (over x, core).
Axes of the slice: x: 4, y: 4, z: 4, core: 2. Of those that a mesh axis runs over, the one named last changes fastest.
Arguments:
- tokens: bfloat16 [4, 4096, 5120], P('pipe', ('dp', 'expert')), may hold values from -6 to 6
- cotangent: bfloat16 [4, 4096, 5120], P('pipe', ('dp', 'expert')), may hold values from -6 to 6
- gain: float32 [4, 5120], P('pipe'), may hold values from 0.1 to 1.9
- w_gate: bfloat16 [4, 8, 5120, 768], P('pipe', 'expert', 'dp'), may hold values from -0.078125 to 0.078125
- w_up: bfloat16 [4, 8, 5120, 768], P('pipe', 'expert', 'dp'), may hold values from -0.078125 to 0.078125
- w_down: bfloat16 [4, 8, 768, 5120], P('pipe', 'expert', None, 'dp'), may hold values from -0.21875 to 0.21875
- route: int32 [4, 4, 512, 1], P('pipe', None, ('dp', 'expert')), may hold values from 0 to 7; in each aligned block of 16 rows (0 to 15, 16 to 31, ..., all dimensions but the last counted through in order) at most 3 rows name the same one
Outputs:
- out_tokens: bfloat16 [4, 4096, 5120], P('pipe', ('dp', 'expert'))
- grad_tokens: bfloat16 [4, 4096, 5120], P('pipe', ('dp', 'expert'))
- grad_gain: float32 [4, 5120], P('pipe')
- grad_gate: bfloat16 [4, 8, 5120, 768], P('pipe', 'expert', 'dp')
- grad_up: bfloat16 [4, 8, 5120, 768], P('pipe', 'expert', 'dp')
- grad_down: bfloat16 [4, 8, 768, 5120], P('pipe', 'expert', None, 'dp')
Inputs may be any that keep to these rules, and one draw needn't show every extreme that they name: route[l, m, t, 0] is the expert of tile t at layer l for micro-batch m. Among the 16 tiles of one device for one layer and one micro-batch (aligned blocks), no expert is named more than 3 times; every expert is named somewhere.
All inputs are finite; a program needn't handle non-finite values.
Results may differ from a plain program's by a relative error of at most 0.034.
Values may be sent and summed in bfloat16 or wider, within the bound.
A program may use at most 128 MiB of HBM per device.

v0:
```python
import jax
import jax.numpy as jnp
from jax import lax
from jax.sharding import PartitionSpec as P

TILE = 8
PASSES = 2


epsilon = 1e-06


def shifted(block, axis, distance):
    devices = range(lax.axis_size(axis))
    route = [((i - distance) % len(devices), i) for i in devices]
    return lax.ppermute(block, axis, route)


def contract_last(former, latter):
    return lax.dot_general(
        former, latter, (((1,), (1,)), ((), ())), preferred_element_type=jnp.float32
    )


def contract_first(former, latter):
    return lax.dot_general(
        former, latter, (((0,), (0,)), ((), ())), preferred_element_type=jnp.float32
    )


def normalize(hidden, gain_row):
    widened = hidden.astype(jnp.float32)
    inverse = lax.rsqrt(jnp.mean(widened * widened, axis=-1, keepdims=True) + epsilon)
    scaled = widened * inverse
    return ((scaled * gain_row).astype(jnp.bfloat16), scaled, inverse)


def slot_matrix(route_now, expert_count, capacity):
    tile_count = route_now.shape[0]
    expert_ids = jnp.arange(expert_count, dtype=jnp.int32)
    member = (route_now[None, :] == expert_ids[:, None]).astype(jnp.int32)
    earlier = jnp.cumsum(member, axis=1) - member
    rank_ids = jnp.arange(capacity, dtype=jnp.int32)
    placed = member[:, None, :] * (earlier[:, None, :] == rank_ids[None, :, None]).astype(jnp.int32)
    return placed.reshape(expert_count * capacity, tile_count)


def into_slots(placed, rows, tile_rows, dp_count):
    width = rows.shape[-1]
    tile_blocks = rows.reshape(placed.shape[1], tile_rows, dp_count, width // dp_count)
    return jnp.einsum(
        "st,trqd->qsrd",
        placed.astype(jnp.bfloat16),
        tile_blocks,
        preferred_element_type=jnp.float32,
    ).astype(jnp.bfloat16)


def from_slots(placed, slot_rows):
    merged = jnp.einsum(
        "st,qsrd->trqd", placed.astype(jnp.bfloat16), slot_rows, preferred_element_type=jnp.float32
    ).astype(jnp.bfloat16)
    return merged.reshape(merged.shape[0] * merged.shape[1], -1)


def send_out(slot_rows):
    quarter = slot_rows.shape[-1]
    flat = slot_rows.reshape((-1,) + slot_rows.shape[2:])
    arrived = lax.all_to_all(flat, ("dp", "expert"), split_axis=0, concat_axis=0, tiled=True)
    return arrived.reshape(-1, quarter)


def send_back(part_rows, dp_count, tile_rows):
    quarter = part_rows.shape[-1]
    flat = part_rows.reshape(-1, tile_rows, quarter)
    returned = lax.all_to_all(flat, ("dp", "expert"), split_axis=0, concat_axis=0, tiled=True)
    return returned.reshape(dp_count, -1, tile_rows, quarter)


def widen_rounded(values):
    return lax.optimization_barrier(values.astype(jnp.bfloat16)).astype(jnp.float32)


def expert_forward(received, gate_weight, up_weight, down_weight):
    gate_terms = widen_rounded(jnp.dot(received, gate_weight, preferred_element_type=jnp.float32))
    up_terms = widen_rounded(jnp.dot(received, up_weight, preferred_element_type=jnp.float32))
    gate_pre, up_pre = (
        lax.psum(gate_terms.astype(jnp.bfloat16), "dp").astype(jnp.float32),
        lax.psum(up_terms.astype(jnp.bfloat16), "dp").astype(jnp.float32),
    )
    activated = (jax.nn.silu(gate_pre) * up_pre).astype(jnp.bfloat16)
    part_rows = jnp.dot(activated, down_weight, preferred_element_type=jnp.float32).astype(
        jnp.bfloat16
    )
    return (part_rows, (gate_pre, up_pre, activated))


def expert_backward(
    received, grad_recv, kept_state, gate_weight, up_weight, down_weight, grad_sums
):
    gate_pre, up_pre, activated = kept_state
    grad_terms = widen_rounded(contract_last(grad_recv, down_weight))
    grad_act = lax.psum(grad_terms.astype(jnp.bfloat16), "dp").astype(jnp.float32)
    sigmoid_gate = jax.nn.sigmoid(gate_pre)
    silu_gate = gate_pre * sigmoid_gate
    grad_gate_pre = (
        grad_act * up_pre * sigmoid_gate * (1.0 + gate_pre * (1.0 - sigmoid_gate))
    ).astype(jnp.bfloat16)
    grad_up_pre = (grad_act * silu_gate).astype(jnp.bfloat16)
    back_rows = (
        contract_last(grad_gate_pre, gate_weight) + contract_last(grad_up_pre, up_weight)
    ).astype(jnp.bfloat16)
    grad_gate = grad_sums[0] + contract_first(received, grad_gate_pre)
    grad_up = grad_sums[1] + contract_first(received, grad_up_pre)
    grad_down = grad_sums[2] + contract_first(activated, grad_recv)
    return (back_rows, (grad_gate, grad_up, grad_down))


def body(tokens, cotangent, gain, w_gate, w_up, w_down, route):
    pipe_count = lax.axis_size("pipe")
    dp_count = lax.axis_size("dp")
    expert_count = lax.axis_size("expert")
    section_index = lax.axis_index("pipe")
    gain_row = gain[0]
    gate_weight = w_gate[0, 0]
    up_weight = w_up[0, 0]
    down_weight = w_down[0, 0]
    route_table = route[0, :, :, 0]
    tile_count = route_table.shape[1]
    capacity = max(2, 3 * tile_count // (2 * expert_count))
    hidden = tokens[0]
    saved_ticks = []
    out_rows = hidden
    for pass_index in range(PASSES):
        micro_index = (section_index - pass_index + pipe_count) % pipe_count
        route_now = lax.dynamic_index_in_dim(route_table, micro_index, 0, keepdims=False)
        placed = slot_matrix(route_now, expert_count, capacity)
        normed, scaled, inverse = normalize(hidden, gain_row)
        received = send_out(into_slots(placed, normed, TILE, dp_count))
        part_rows, kept_state = expert_forward(received, gate_weight, up_weight, down_weight)
        ffn_rows = from_slots(placed, send_back(part_rows, dp_count, TILE))
        new_hidden = (hidden.astype(jnp.float32) + ffn_rows.astype(jnp.float32)).astype(
            jnp.bfloat16
        )
        saved_ticks.append((placed, scaled, inverse, received, kept_state))
        if pass_index + 1 < PASSES:
            hidden = shifted(new_hidden, "pipe", 1)
        else:
            out_rows = new_hidden
    grad_rows = cotangent[0]
    grad_sums = (
        jnp.zeros(gate_weight.shape, jnp.float32),
        jnp.zeros(up_weight.shape, jnp.float32),
        jnp.zeros(down_weight.shape, jnp.float32),
    )
    gain_sum = jnp.zeros(gain_row.shape, jnp.float32)
    entry_grad = grad_rows
    for pass_index in reversed(range(PASSES)):
        placed, scaled, inverse, received, kept_state = saved_ticks[pass_index]
        grad_recv = send_out(into_slots(placed, grad_rows, TILE, dp_count))
        back_rows, grad_sums = expert_backward(
            received, grad_recv, kept_state, gate_weight, up_weight, down_weight, grad_sums
        )
        grad_normed = from_slots(placed, send_back(back_rows, dp_count, TILE)).astype(jnp.float32)
        gain_sum = gain_sum + jnp.sum(grad_normed * scaled, axis=0)
        grad_scaled = grad_normed * gain_row
        grad_wide = inverse * (
            grad_scaled - scaled * jnp.mean(grad_scaled * scaled, axis=-1, keepdims=True)
        )
        grad_in = (grad_rows.astype(jnp.float32) + grad_wide).astype(jnp.bfloat16)
        if pass_index > 0:
            grad_rows = shifted(grad_in, "pipe", -1)
        else:
            entry_grad = grad_in
    gain_total = lax.psum(gain_sum, ("dp", "expert"))
    return (
        out_rows[None],
        entry_grad[None],
        gain_total[None],
        grad_sums[0].astype(jnp.bfloat16)[None, None],
        grad_sums[1].astype(jnp.bfloat16)[None, None],
        grad_sums[2].astype(jnp.bfloat16)[None, None],
    )


def solution(mesh):
    placed = (
        P("pipe", ("dp", "expert"), None),
        P("pipe", ("dp", "expert"), None),
        P("pipe", None),
        P("pipe", "expert", "dp", None),
        P("pipe", "expert", "dp", None),
        P("pipe", "expert", None, "dp"),
        P("pipe", None, ("dp", "expert"), None),
    )
    return jax.shard_map(
        body,
        mesh=mesh,
        in_specs=placed,
        out_specs=(
            P("pipe", ("dp", "expert"), None),
            P("pipe", ("dp", "expert"), None),
            P("pipe", None),
            P("pipe", "expert", "dp", None),
            P("pipe", "expert", "dp", None),
            P("pipe", "expert", None, "dp"),
        ),
        check_vma=False,
    )
```

profile of v0, /device:TPU:1, one launch (start us, length us, event | category | flops | bytes accessed | tf_op | source)
XLA Modules:
  0.0 708.8 jit_solution(6603323839218652019)
XLA Ops:
  13.2 35.5 %all_to_all.40 = bf16[96,8,1280]{2,1,0:T(8,128)(2,1)S(1)} all-to-all(bf16[96,8,1280]{2,1,0:T(8,128)(2,1)S(1)} %copy.49), channel_id=1, replica_groups=mesh['dp'=4,'pipe'=4,'expert'=8] {'dp','expert'}, dimensions={0} | all-to-all | bytes 3932160 | tf_op jit(solution)/shard_map/all_to_all | solution.py:69
  54.2 61.7 %all-reduce.10.cloned.1.call-done = (bf16[768,768]{1,0:T(8,128)(2,1)}, bf16[768,768]{1,0:T(8,128)(2,1)}) async-done(((bf16[768,768]{1,0:T(8,128)(2,1)}, bf16[768,768]{1,0:T(8,128)(2,1)}), (bf16[768,768]{1,0:T(8,128)(2,1)}, bf16[768,768]{1,0:T(8,128)(2,1)})) %all-reduce.10.cloned.1.call-update) | async-done | bytes 2359312 | tf_op jit(solution)/shard_map/psum | solution.py:89
  119.7 32.9 %all_to_all.41 = bf16[96,8,1280]{2,1,0:T(8,128)(2,1)S(1)} all-to-all(bf16[96,8,1280]{2,1,0:T(8,128)(2,1)S(1)} %fusion.12), channel_id=1, replica_groups=mesh['dp'=4,'pipe'=4,'expert'=8] {'dp','expert'}, dimensions={0} | all-to-all | bytes 3932160 | tf_op jit(solution)/shard_map/all_to_all | solution.py:76
  163.8 5.1 all-to-all-start.4
  169.0 19.6 %collective-permute-done = bf16[128,5120]{1,0:T(8,128)(2,1)} collective-permute-done((bf16[128,5120]{1,0:T(8,128)(2,1)}, bf16[128,5120]{1,0:T(8,128)(2,1)}, u32[]{:S(2)}, u32[]{:S(2)}) %collective-permute-start) | collective-permute-done | bytes 1310752 | tf_op jit(solution)/shard_map/ppermute | solution.py:16
  195.4 6.7 all-to-all-start.2
  202.2 4.3 fusion.114
  206.4 22.1 %all-to-all-done.2 = bf16[96,8,1280]{2,1,0:T(8,128)(2,1)} async-done(((bf16[96,8,1280]{2,1,0:T(8,128)(2,1)}), bf16[96,8,1280]{2,1,0:T(8,128)(2,1)}, u32[]{:S(2)}, u32[]{:S(2)}) %all-to-all-start.2) | async-done | bytes 1966112 | tf_op jit(solution)/shard_map/all_to_all | solution.py:69
  228.5 5.0 fusion.104
  233.5 4.3 fusion.109
  237.8 81.3 %all-reduce.8.cloned.1.call-done = (bf16[768,768]{1,0:T(8,128)(2,1)}, bf16[768,768]{1,0:T(8,128)(2,1)}, bf16[768,768]{1,0:T(8,128)(2,1)}) async-done(((bf16[768,768]{1,0:T(8,128)(2,1)}, bf16[768,768]{1,0:T(8,128)(2,1)}, bf16[768,768]{1,0:T(8,128)(2,1)}), (bf16[768,768]{1,0:T(8,128)(2,1)}, bf16[768,768]{1,0:T(8,128)(2,1)}, bf16[768,768]{1,0:T(8,128)(2,1)})) %all-reduce.8.cloned.1.call-update) | async-done | bytes 3538960 | tf_op jit(solution)/shard_map/psum | solution.py:89
  319.1 5.0 fusion.13
  324.1 6.3 all-to-all-start.3
  330.5 5.3 fusion.81
  339.2 17.6 %all-to-all-done.3 = bf16[96,8,1280]{2,1,0:T(8,128)(2,1)} async-done(((bf16[96,8,1280]{2,1,0:T(8,128)(2,1)}), bf16[96,8,1280]{2,1,0:T(8,128)(2,1)}, u32[]{:S(2)}, u32[]{:S(2)}) %all-to-all-start.3) | async-done | bytes 1966112 | tf_op jit(solution)/shard_map/all_to_all | solution.py:76
  356.8 6.7 all-to-all-start.5
  369.2 20.7 %all-to-all-done.5 = bf16[96,8,1280]{2,1,0:T(8,128)(2,1)} async-done(((bf16[96,8,1280]{2,1,0:T(8,128)(2,1)}), bf16[96,8,1280]{2,1,0:T(8,128)(2,1)}, u32[]{:S(2)}, u32[]{:S(2)}) %all-to-all-start.5) | async-done | bytes 1966112 | tf_op jit(solution)/shard_map/all_to_all | solution.py:76
  402.9 25.7 %collective-permute-done.1 = bf16[128,5120]{1,0:T(8,128)(2,1)} collective-permute-done((bf16[128,5120]{1,0:T(8,128)(2,1)S(1)}, bf16[128,5120]{1,0:T(8,128)(2,1)}, u32[]{:S(2)}, u32[]{:S(2)}) %collective-permute-start.1) | collective-permute-done | bytes 1310752 | tf_op jit(solution)/shard_map/ppermute | solution.py:16
  436.8 8.3 %all-to-all-start.6 = ((bf16[96,8,1280]{2,1,0:T(8,128)(2,1)}), bf16[96,8,1280]{2,1,0:T(8,128)(2,1)}, u32[]{:S(2)}, u32[]{:S(2)}) async-start(bf16[96,8,1280]{2,1,0:T(8,128)(2,1)} %copy.67), calls=%async_computation.6 | async-start | bytes 3932160 | tf_op jit(solution)/shard_map/all_to_all | solution.py:69
  449.4 5.9 fusion.62
  455.3 16.2 %all-to-all-done.6 = bf16[96,8,1280]{2,1,0:T(8,128)(2,1)} async-done(((bf16[96,8,1280]{2,1,0:T(8,128)(2,1)}), bf16[96,8,1280]{2,1,0:T(8,128)(2,1)}, u32[]{:S(2)}, u32[]{:S(2)}) %all-to-all-start.6) | async-done | bytes 1966112 | tf_op jit(solution)/shard_map/all_to_all | solution.py:69
  471.6 4.3 fusion.119
  475.9 6.1 fusion.58
  482.0 5.4 fusion.64
  487.5 33.7 %all-reduce.6.cloned.1.call-done = bf16[768,768]{1,0:T(8,128)(2,1)} async-done(((bf16[768,768]{1,0:T(8,128)(2,1)}), bf16[768,768]{1,0:T(8,128)(2,1)}) %all-reduce.6.cloned.1.call-update) | async-done | bytes 1179664 | tf_op jit(solution)/shard_map/psum | solution.py:103
  521.1 5.3 fusion.79
  530.0 8.3 %all-to-all-start.7 = ((bf16[96,8,1280]{2,1,0:T(8,128)(2,1)}), bf16[96,8,1280]{2,1,0:T(8,128)(2,1)}, u32[]{:S(2)}, u32[]{:S(2)}) async-start(bf16[96,8,1280]{2,1,0:T(8,128)(2,1)} %fusion.15), calls=%async_computation.7 | async-start | bytes 3932160 | tf_op jit(solution)/shard_map/all_to_all | solution.py:76
  538.4 6.7 fusion.18
  551.6 13.1 %all-to-all-done.7 = bf16[96,8,1280]{2,1,0:T(8,128)(2,1)} async-done(((bf16[96,8,1280]{2,1,0:T(8,128)(2,1)}), bf16[96,8,1280]{2,1,0:T(8,128)(2,1)}, u32[]{:S(2)}, u32[]{:S(2)}) %all-to-all-start.7) | async-done | bytes 1966112 | tf_op jit(solution)/shard_map/all_to_all | solution.py:76
  564.7 5.9 multiply_reduce_fusion
  570.6 121.9 %psum.55 = f32[1,5120]{1,0:T(1,128)} all-reduce(f32[1,5120]{1,0:T(1,128)S(1)} %bitcast.217), channel_id=1, replica_groups=mesh['dp'=4,'pipe'=4,'expert'=8] {'dp','expert'}, use_global_device_ids=true, to_apply=%region_14.15 | all-reduce | flops 5120 | bytes 40960 | tf_op jit(solution)/shard_map/psum | solution.py:175
  698.1 4.0 fusion.124
  (115 shorter events, 83.5 us)
Async XLA Ops:
  7.2 108.7 %copy-start = (bf16[1,1,768,1280]{3,2,1,0:T(8,128)(2,1)S(1)}, bf16[1,1,768,1280]{3,2,1,0:T(8,128)(2,1)}, u32[]{:S(2)}) copy-start(bf16[1,1,768,1280]{3,2,1,0:T(8,128)(2,1)} %param.12) | copy-start | bytes 5898244
  7.2 2.8 copy-start.1
  7.2 108.7 %all-reduce.10.cloned.1.call-start = ((), (), s32[]{:S(2)}) async-start(), calls=%async_computation.10 | async-start | bytes 4718592 | tf_op jit(solution)/shard_map/psum | solution.py:89
  13.2 35.5 %copy-start.7 = (bf16[1,1,1280,768]{3,2,1,0:T(8,128)(2,1)S(1)}, bf16[1,1,1280,768]{3,2,1,0:T(8,128)(2,1)}, u32[]{:S(2)}) copy-start(bf16[1,1,1280,768]{3,2,1,0:T(8,128)(2,1)} %param.10) | copy-start | bytes 5898244
  48.8 2.7 copy-start.8
  156.6 31.9 %collective-permute-start = (bf16[128,5120]{1,0:T(8,128)(2,1)}, bf16[128,5120]{1,0:T(8,128)(2,1)}, u32[]{:S(2)}, u32[]{:S(2)}) collective-permute-start(bf16[128,5120]{1,0:T(8,128)(2,1)} %fusion.29), channel_id=1, source_target_pairs={{24,0},{0,8},{8,16},{16,24},{25,1},{1,9},{9,17},{17,25},{26,2},{2,... | collective-permute-start | bytes 3932168 | tf_op jit(solution)/shard_map/ppermute | solution.py:16
  163.8 26.4 %copy-start.6 = (f32[1,5120]{1,0:T(1,128)S(1)}, f32[1,5120]{1,0:T(1,128)}, u32[]{:S(2)}) copy-start(f32[1,5120]{1,0:T(1,128)} %param.9) | copy-start | bytes 61444
  163.8 31.6 %all-to-all-start.4 = ((bf16[96,8,1280]{2,1,0:T(8,128)(2,1)}), bf16[96,8,1280]{2,1,0:T(8,128)(2,1)}, u32[]{:S(2)}, u32[]{:S(2)}) async-start(bf16[96,8,1280]{2,1,0:T(8,128)(2,1)} %copy.61), calls=%async_computation.4 | async-start | bytes 3932160 | tf_op jit(solution)/shard_map/all_to_all | solution.py:69
  195.4 33.2 %all-to-all-start.2 = ((bf16[96,8,1280]{2,1,0:T(8,128)(2,1)}), bf16[96,8,1280]{2,1,0:T(8,128)(2,1)}, u32[]{:S(2)}, u32[]{:S(2)}) async-start(bf16[96,8,1280]{2,1,0:T(8,128)(2,1)} %copy.55), calls=%async_computation.2 | async-start | bytes 3932160 | tf_op jit(solution)/shard_map/all_to_all | solution.py:69
  202.1 117.0 %all-reduce.8.cloned.1.call-start = ((), (), s32[]{:S(2)}) async-start(), calls=%async_computation.9 | async-start | bytes 7077888 | tf_op jit(solution)/shard_map/psum | solution.py:89
  228.5 5.0 copy-start.9
  324.1 32.7 %all-to-all-start.3 = ((bf16[96,8,1280]{2,1,0:T(8,128)(2,1)}), bf16[96,8,1280]{2,1,0:T(8,128)(2,1)}, u32[]{:S(2)}, u32[]{:S(2)}) async-start(bf16[96,8,1280]{2,1,0:T(8,128)(2,1)} %fusion.13), calls=%async_computation.3 | async-start | bytes 3932160 | tf_op jit(solution)/shard_map/all_to_all | solution.py:76
  330.4 5.3 copy-start.10
  330.4 5.3 copy-start.16
  330.4 5.3 copy-start.18
  356.8 33.1 %all-to-all-start.5 = ((bf16[96,8,1280]{2,1,0:T(8,128)(2,1)}), bf16[96,8,1280]{2,1,0:T(8,128)(2,1)}, u32[]{:S(2)}, u32[]{:S(2)}) async-start(bf16[96,8,1280]{2,1,0:T(8,128)(2,1)} %fusion.14), calls=%async_computation.5 | async-start | bytes 3932160 | tf_op jit(solution)/shard_map/all_to_all | solution.py:76
  400.2 28.3 %collective-permute-start.1 = (bf16[128,5120]{1,0:T(8,128)(2,1)S(1)}, bf16[128,5120]{1,0:T(8,128)(2,1)}, u32[]{:S(2)}, u32[]{:S(2)}) collective-permute-start(bf16[128,5120]{1,0:T(8,128)(2,1)S(1)} %get-tuple-element.15), channel_id=1, source_target_pairs={{8,0},{16,8},{24,16},{0,24},{9,1},{17,9},{25,17},{1,25},{10,2},{18... | collective-permute-start | bytes 3932168 | tf_op jit(solution)/shard_map/ppermute | solution.py:16
  436.8 34.7 %all-to-all-start.6 = ((bf16[96,8,1280]{2,1,0:T(8,128)(2,1)}), bf16[96,8,1280]{2,1,0:T(8,128)(2,1)}, u32[]{:S(2)}, u32[]{:S(2)}) async-start(bf16[96,8,1280]{2,1,0:T(8,128)(2,1)} %copy.67), calls=%async_computation.6 | async-start | bytes 3932160 | tf_op jit(solution)/shard_map/all_to_all | solution.py:69
  445.2 76.0 %all-reduce.6.cloned.1.call-start = ((), (), s32[]{:S(2)}) async-start(), calls=%async_computation.8 | async-start | bytes 2359296 | tf_op jit(solution)/shard_map/psum | solution.py:103
  475.9 6.2 copy-start.15
  475.9 6.1 copy-start.17
  475.9 6.1 copy-start.19
  521.1 5.3 copy-start.11
  521.1 5.3 copy-start.13
  521.1 5.3 copy-start.20
  530.0 34.7 %all-to-all-start.7 = ((bf16[96,8,1280]{2,1,0:T(8,128)(2,1)}), bf16[96,8,1280]{2,1,0:T(8,128)(2,1)}, u32[]{:S(2)}, u32[]{:S(2)}) async-start(bf16[96,8,1280]{2,1,0:T(8,128)(2,1)} %fusion.15), calls=%async_computation.7 | async-start | bytes 3932160 | tf_op jit(solution)/shard_map/all_to_all | solution.py:76
  538.3 6.8 copy-start.5
  538.3 6.8 copy-start.14
  538.4 6.8 copy-start.21
  538.4 6.8 copy-start.22
  545.1 3.2 copy-start.12
  545.1 3.2 copy-start.23
  (3 other events, 7.7 us)
Sparse Core Ops, SparseCore 0:
  54.3 61.5 all-reduce.9
  237.9 81.1 all-reduce.7
  476.0 45.1 all-reduce.5
where the time goes:
time: 723 us; the launch traced here: 709 us
  waiting for transfers between devices  312 us (43%)
  blocking collectives  190 us (26%)
  matrix products  98 us (14%)
  starting transfers between devices  46.4 us (6%)
  local copies, waits for them, and re-layouts  29.4 us (4%)
  other arithmetic  18.6 us (3%)
  between operations  14.4 us (2%)
    psum x2, waiting for transfers between devices, expert_forward(): lax.psum(up_terms.astype(jnp.bfloat16), 'dp').astype(jnp.float32)  143 us
    psum x1, blocking collectives, body(): gain_total = lax.psum(gain_sum, ('dp', 'expert'))  122 us
    all_to_all x3, waiting for transfers between devices, send_back(): lax.all_to_all(flat, ('dp', 'expert'), split_axis=0, concat_axis=0, tiled...  51.4 us
    ppermute x2, waiting for transfers between devices, shifted(): return lax.ppermute(block, axis, route)  45.3 us
    all_to_all x3, waiting for transfers between devices, send_out(): lax.all_to_all(flat, ('dp', 'expert'), split_axis=0, concat_axis=0, tiled...  38.4 us
    all_to_all x1, blocking collectives, send_out(): lax.all_to_all(flat, ('dp', 'expert'), split_axis=0, concat_axis=0, tiled...  35.5 us
    psum x1, waiting for transfers between devices, expert_backward(): lax.psum(grad_terms.astype(jnp.bfloat16), 'dp').astype(jnp.float32)  33.7 us
    all_to_all x1, blocking collectives, send_back(): lax.all_to_all(flat, ('dp', 'expert'), split_axis=0, concat_axis=0, tiled...  32.9 us
  transfers between devices with their start and end apart: 11, of which 11 were waited for; matrix products, arithmetic and copies ran while one was open for 9% of the time, Pallas kernels for 0%

commit v1 on v0

v1 whole, which is shorter than its diff:
```python
import functools
import math

import jax
import jax.numpy as jnp
from jax import lax
from jax.experimental import pallas as pl
from jax.experimental.pallas import tpu as pltpu
from jax.sharding import PartitionSpec as P

TILE = 8
CAP = 3
PASSES = 2
WIDTH = 256
epsilon = 1e-06
F32 = jnp.float32
BF16 = jnp.bfloat16


def kernel(
    sizes,
    dest, tok, cot, gain, wg, wu, wd,
    out_tok, grad_tok, gain_out, gg, gu, gd,
    tokc, cotc, hid1, grad0, norm, wgu, wdc, dest_all, place, back,
    yin, xout, xin, acc, gate_up, act, act_t, grad_act,
    rs_f, rs_b, one_f, one_b, two_f, two_b,
    ret_out, ret_in, yret_out, yret_in, inverse, mean_acc, gain_acc, gain_dp, gain_ex, gain_all,
    load_sem, store_sem, dest_s, dest_r, y_s, y_r, x_s, x_r, rx_s, rx_r, ry_s, ry_r,
    z_s, z_r, ar_s, one_r, two_r, ag_r, gain_s, gain_r,
):
    nd, npipe, ne, rows, width, hidden = sizes
    quarter = width // nd
    kc = min(WIDTH, quarter)
    nk = quarter // kc
    block = nd * CAP * TILE
    total = ne * block
    half_ne = ne // 2
    group = total // 2
    part = group // nd
    half = part // 2
    q, p, e = lax.axis_index("dp"), lax.axis_index("pipe"), lax.axis_index("expert")
    chip, core = e // 2, lax.rem(e, 2)
    place_e = core * half_ne + chip
    q_up, q_down, q_far = lax.rem(q + 1, nd), lax.rem(q + nd - 1, nd), lax.rem(q + 2, nd)
    p_up, p_down = lax.rem(p + 1, npipe), lax.rem(p + npipe - 1, npipe)

    def send(src, dst, ssem, rsem, **where):
        pltpu.make_async_remote_copy(
            src_ref=src, dst_ref=dst, send_sem=ssem, recv_sem=rsem,
            device_id=where, device_id_type=pl.DeviceIdType.MESH,
        ).start()

    def drain(ref, sem):
        pltpu.make_async_copy(ref, ref, sem).wait()

    def loop(count, step):
        lax.fori_loop(0, count, lambda i, c: (step(i), c)[1], 0)

    def at(i, size):
        return pl.ds(pl.multiple_of(i * size, size), size)

    for k in range(nk):
        for j in range(nd):
            cols = pl.ds(j * quarter + k * kc, kc)
            pltpu.make_async_copy(tok.at[:, cols], tokc.at[k, j], load_sem.at[0]).start()
    pltpu.make_async_copy(wg, wgu.at[:, 0:hidden], load_sem.at[1]).start()
    pltpu.make_async_copy(wu, wgu.at[:, hidden : 2 * hidden], load_sem.at[1]).start()
    for k in range(nk):
        pltpu.make_async_copy(wd.at[:, pl.ds(k * kc, kc)], wdc.at[k], load_sem.at[2]).start()
    for k in range(nk):
        for j in range(nd):
            cols = pl.ds(j * quarter + k * kc, kc)
            pltpu.make_async_copy(cot.at[:, cols], cotc.at[k, j], load_sem.at[3]).start()

    barrier = pltpu.get_barrier_semaphore()

    def greet(**where):
        pl.semaphore_signal(barrier, inc=1, device_id=where, device_id_type=pl.DeviceIdType.MESH)

    for d in range(1, nd):
        greet(dp=lax.rem(q + d, nd))
    for d in range(1, ne):
        greet(expert=lax.rem(e + d, ne))
    greet(pipe=p_up)
    greet(pipe=p_down)

    drain(tokc, load_sem.at[0])

    def squares(ref, k, before):
        for j in range(nd):
            wide = ref[k, j].astype(F32)
            before = before + jnp.sum(wide * wide, axis=-1, keepdims=True)
        return before

    def normalize(t, ref, total_squares):
        inverse[t] = lax.rsqrt(total_squares / width + epsilon)

        def step(k):
            for j in range(nd):
                norm[k, j] = (ref[k, j].astype(F32) * inverse[t] * gain[k, j]).astype(BF16)

        loop(nk, step)

    none = jnp.zeros((rows, 1), F32)
    normalize(0, tokc, lax.fori_loop(0, nk, lambda k, c: squares(tokc, k, c), none))
    pl.semaphore_wait(barrier, nd - 1 + ne - 1 + 2)

    for d in range(1, nd):
        send(dest, dest_all.at[q], dest_s, dest_r, dp=lax.rem(q + d, nd))
    dest_all[q] = dest[...]

    def build_places():
        drain(dest_all.at[0 : nd - 1], dest_r)
        slot_ids = lax.broadcasted_iota(jnp.int32, (total, rows), 0).astype(F32)
        for t in range(PASSES):
            for s in range(nd):
                hot = jnp.where(slot_ids == dest_all[s, t, 0:1, :], 1.0, 0.0).astype(F32)
                place[t, :, s * rows : (s + 1) * rows] = hot.astype(BF16)
                back[t, s * rows : (s + 1) * rows, :] = hot.T.astype(BF16)

    tall = total // 3

    def y_send(ph, st, src, k):
        for d in range(1, nd):
            j = lax.rem(q + d, nd)
            send(src.at[k, j], yin.at[st, k, at(q, rows)], y_s.at[ph, k], y_r.at[ph, k], dp=j)
        yin[st, k, at(q, rows), :] = src[k, q]

    def x_send(ph, st, t, k):
        drain(yin.at[st, k, 0 : (nd - 1) * rows], y_r.at[ph, k])

        def some(m):
            xout[k, at(m, tall), :] = jnp.dot(
                place[t, at(m, tall), :], yin[st, k], preferred_element_type=F32
            ).astype(BF16)

        loop(3, some)
        for d in range(1, ne):
            o = lax.rem(e + d, ne)
            send(xout.at[k, at(o, block)], xin.at[ph, k, at(place_e, block)], x_s.at[ph, k], x_r.at[ph, k], expert=o)
        xin[ph, k, at(place_e, block), :] = xout[k, at(e, block), :]

    def forward_chunk(ph, k):
        drain(xin.at[ph, k, 0 : (ne - 1) * block], x_r.at[ph, k])

        def some(m):
            acc[at(m, tall), :] += jnp.dot(
                xin[ph, k, at(m, tall), :], wgu[at(k, kc), :], preferred_element_type=F32
            )

        loop(3, some)

    def backward_chunk(ph, k):
        drain(xin.at[ph, k, 0 : (ne - 1) * block], x_r.at[ph, k])

        def some(m):
            acc[at(m, tall), 0:hidden] += lax.dot_general(
                xin[ph, k, at(m, tall), :], wdc[k], (((1,), (1,)), ((), ())), preferred_element_type=F32
            )

        loop(3, some)

    def dispatch(ph, st, t, src, chunk, arrive=None, early=None):
        if arrive is None:
            loop(nk, lambda k: y_send(ph, st, src, k))
        if early is not None:
            early()
        acc[...] = jnp.zeros_like(acc)
        ahead = 0 if arrive is None else 1

        def step(i):
            if arrive is not None:

                @pl.when(i < nk)
                def _():
                    arrive(i)
                    y_send(ph, st, src, i)

            @pl.when((i >= ahead) & (i < nk + ahead))
            def _():
                x_send(ph, st, t, i - ahead)

            @pl.when(i >= ahead + 1)
            def _():
                chunk(ph, i - ahead - 1)

        loop(nk + 1 + ahead, step)

        def settle(k):
            drain(yin.at[st, k, 0 : (nd - 1) * rows], y_s.at[ph, k])
            drain(xout.at[k, 0 : (ne - 1) * block], x_s.at[ph, k])

        loop(nk, settle)

    def all_sum(ph, src, dst, one, two, columns):
        def span(g, b, h):
            return pl.ds(pl.multiple_of(g * group + b * part + h * half, half), half)

        def open_(g):
            send(src.at[span(g, q_far, 0)], one.at[g, 0], ar_s.at[ph, g, 0], one_r.at[ph, g, 0], dp=q_down)
            send(src.at[span(g, q_far, 1)], one.at[g, 1], ar_s.at[ph, g, 1], one_r.at[ph, g, 1], dp=q_up)
            send(src.at[span(g, q_down, 1)], two.at[g, 0, 1], ar_s.at[ph, g, 2], two_r.at[ph, g, 0, 1], dp=q_down)
            send(src.at[span(g, q_up, 0)], two.at[g, 1, 0], ar_s.at[ph, g, 3], two_r.at[ph, g, 1, 0], dp=q_up)

        def middle(g):
            for side, b in ((0, q_down), (1, q_up)):
                drain(one.at[g, side], one_r.at[ph, g, side])
                there = span(g, b, side)
                src[there, :] = (src[there, :].astype(F32) + one[g, side].astype(F32)).astype(BF16)
                send(src.at[there], two.at[g, side, side], ar_s.at[ph, g, 4 + side], two_r.at[ph, g, side, side], dp=b)

        def own(g):
            for h in range(2):
                for side in range(2):
                    drain(two.at[g, side, h], two_r.at[ph, g, side, h])
                mine = span(g, q, h)
                dst[mine, :] = (
                    src[mine, :].astype(F32) + two[g, 0, h].astype(F32) + two[g, 1, h].astype(F32)
                ).astype(BF16)
            for i in range(2):
                up, down = span(g, q, i), span(g, q, 1 - i)
                send(dst.at[up], dst.at[up], ar_s.at[ph, g, 6 + i], ag_r.at[ph, g, 0, i], dp=q_up)
                send(dst.at[down], dst.at[down], ar_s.at[ph, g, 8 + i], ag_r.at[ph, g, 1, 1 - i], dp=q_down)

        def pass_on(g):
            first, second = span(g, q_down, 0), span(g, q_up, 1)
            drain(dst.at[first], ag_r.at[ph, g, 0, 0])
            send(dst.at[first], dst.at[first], ar_s.at[ph, g, 10], ag_r.at[ph, g, 2, 0], dp=q_up)
            drain(dst.at[second], ag_r.at[ph, g, 1, 1])
            send(dst.at[second], dst.at[second], ar_s.at[ph, g, 11], ag_r.at[ph, g, 2, 1], dp=q_down)

        def close(g):
            drain(dst.at[span(g, q_down, 1)], ag_r.at[ph, g, 0, 1])
            drain(dst.at[span(g, q_up, 0)], ag_r.at[ph, g, 1, 0])
            drain(dst.at[span(g, q_far, 0)], ag_r.at[ph, g, 2, 0])
            drain(dst.at[span(g, q_far, 1)], ag_r.at[ph, g, 2, 1])

        def settle():
            for g in range(2):
                for i in range(12):
                    drain(src.at[0:half], ar_s.at[ph, g, i])

        return open_, middle, own, pass_on, close, settle

    def round_into(src, columns, g):
        def some(m):
            there = pl.ds(pl.multiple_of(g * group + m * half, half), half)
            src[there, :] = acc[there, 0:columns].astype(BF16)

        loop(group // half, some)

    def ret_send(ph, st, g, k):
        for i in range(half_ne):
            c = lax.rem(chip + i, half_ne)
            there = pl.ds(pl.multiple_of(g * group + c * block, block), block)
            landing = ret_in.at[st, k, at(e, block)]
            if i == 0:

                @pl.when(core != g)
                def _():
                    send(ret_out.at[k, there], landing, rx_s.at[ph, k], rx_r.at[ph, k], expert=2 * c + g)

                @pl.when(core == g)
                def _():
                    ret_in[st, k, at(e, block), :] = ret_out[k, there, :]
            else:
                send(ret_out.at[k, there], landing, rx_s.at[ph, k], rx_r.at[ph, k], expert=2 * c + g)

    short = nd * rows // 2

    def collect(ph, st, t, k):
        drain(ret_in.at[st, k, 0 : (ne - 1) * block], rx_r.at[ph, k])

        def some(m):
            yret_out[k, at(m, short), :] = jnp.dot(
                back[t, at(m, short), :], ret_in[st, k], preferred_element_type=F32
            ).astype(BF16)

        loop(2, some)
        for d in range(1, nd):
            j = lax.rem(q + d, nd)
            send(yret_out.at[k, at(j, rows)], yret_in.at[st, k, q], ry_s.at[ph, k], ry_r.at[ph, k], dp=j)
        yret_in[st, k, q] = yret_out[k, at(q, rows), :]

    def landed(ph, st, k):
        drain(yret_in.at[st, k, 0 : nd - 1], ry_r.at[ph, k])

    def settle_return(ph):
        def step(k):
            drain(ret_out.at[k, 0 : (ne - 1) * block], rx_s.at[ph, k])
            drain(yret_out.at[k, 0 : (nd - 1) * rows], ry_s.at[ph, k])

        loop(nk, step)

    def forward_expert(ph, t):
        open_, middle, own, pass_on, close, settle = all_sum(ph, rs_f, gate_up.at[t], one_f, two_f, 2 * hidden)
        for g in range(2):
            round_into(rs_f, 2 * hidden, g)
            open_(g)
        middle(0)
        middle(1)
        own(0)
        own(1)
        pass_on(0)
        pass_on(1)
        for g in range(2):
            close(g)

            def activate(m):
                there = pl.ds(pl.multiple_of(g * group + m * half, half), half)
                gate = gate_up[t, there, 0:hidden].astype(F32)
                up = gate_up[t, there, hidden : 2 * hidden].astype(F32)
                act[there, :] = (gate * jax.nn.sigmoid(gate) * up).astype(BF16)

            loop(group // half, activate)
            mine = slice(g * group, (g + 1) * group)

            def down(k):
                ret_out[k, mine, :] = jnp.dot(act[mine, :], wdc[k], preferred_element_type=F32).astype(BF16)
                ret_send(ph, 0, g, k)

            loop(nk, down)
        wide = math.gcd(total, 128)
        for m in range(total // wide):
            act_t[t, :, m * wide : (m + 1) * wide] = act[m * wide : (m + 1) * wide, :].T
        settle()

    def forward_return(ph, t, ref):
        def step(i):
            @pl.when(i < nk)
            def _():
                collect(ph, 0, t, i)

            @pl.when(i >= 1)
            def _():
                k = i - 1
                landed(ph, 0, k)
                for j in range(nd):
                    yret_in[0, k, j] = (ref[k, j].astype(F32) + yret_in[0, k, j].astype(F32)).astype(BF16)
                if t == 0:
                    send(yret_in.at[0, k], hid1.at[k], z_s.at[0, k], z_r.at[0, k], pipe=p_up)
                else:
                    for j in range(nd):
                        cols = pl.ds(pl.multiple_of(j * quarter + k * kc, kc), kc)
                        pltpu.make_async_copy(yret_in.at[0, k, j], out_tok.at[:, cols], store_sem.at[0]).start()

        loop(nk + 1, step)
        settle_return(ph)

    def backward_expert(ph, t):
        def pre(m):
            there = pl.ds(pl.multiple_of(m * half, half), half)
            gate = gate_up[t, there, 0:hidden].astype(F32)
            up = gate_up[t, there, hidden : 2 * hidden].astype(F32)
            grad = grad_act[there, :].astype(F32)
            s = jax.nn.sigmoid(gate)
            gate_up[t, there, 0:hidden] = (grad * up * s * (1.0 + gate * (1.0 - s))).astype(BF16)
            gate_up[t, there, hidden : 2 * hidden] = (grad * (gate * s)).astype(BF16)

        for g in range(2):
            lax.fori_loop(g * (group // half), (g + 1) * (group // half), lambda m, c: (pre(m), c)[1], 0)
            mine = slice(g * group, (g + 1) * group)

            def up_(k):
                ret_out[k, mine, :] = lax.dot_general(
                    gate_up[t, mine, :], wgu[at(k, kc), :], (((1,), (1,)), ((), ())), preferred_element_type=F32
                ).astype(BF16)
                ret_send(ph, 1, g, k)

            loop(nk, up_)

    def backward_return(ph, t, ref, grad_ref, beside):
        def terms(k, j):
            u = yret_in[1, k, j].astype(F32)
            return u, ref[k, j].astype(F32) * inverse[t]

        mean_acc[...] = jnp.zeros_like(mean_acc)

        def step(i):
            @pl.when(i < nk)
            def _():
                beside(i)
                collect(ph, 1, t, i)

            @pl.when(i >= 1)
            def _():
                k = i - 1
                landed(ph, 1, k)
                fresh = mean_acc[...]
                for j in range(nd):
                    u, scaled = terms(k, j)
                    both = u * scaled
                    gain_acc[j, k] += jnp.sum(both.reshape(rows // 8, 8, kc), axis=0)
                    fresh = fresh + both * gain[k, j]
                mean_acc[...] = fresh

        loop(nk + 1, step)
        mean = jnp.sum(mean_acc[...], axis=-1, keepdims=True) / width

        def finish(k):
            for j in range(nd):
                u, scaled = terms(k, j)
                wide = inverse[t] * (u * gain[k, j] - scaled * mean)
                yret_in[1, k, j] = (grad_ref[k, j].astype(F32) + wide).astype(BF16)
            if t == 1:
                send(yret_in.at[1, k], grad0.at[k], z_s.at[1, k], z_r.at[1, k], pipe=p_down)
            else:
                for j in range(nd):
                    cols = pl.ds(pl.multiple_of(j * quarter + k * kc, kc), kc)
                    pltpu.make_async_copy(yret_in.at[1, k, j], grad_tok.at[:, cols], store_sem.at[1]).start()

        loop(nk, finish)
        settle_return(ph)

    def weight_grads(k):
        both = jnp.zeros((kc, 2 * hidden), F32)
        for t in range(PASSES):
            both = both + lax.dot_general(
                xin[t, k], gate_up[t], (((0,), (0,)), ((), ())), preferred_element_type=F32
            )
        wgu[at(k, kc), :] = both.astype(BF16)
        pltpu.make_async_copy(wgu.at[at(k, kc), 0:hidden], gg.at[at(k, kc)], store_sem.at[2]).start()
        pltpu.make_async_copy(wgu.at[at(k, kc), hidden : 2 * hidden], gu.at[at(k, kc)], store_sem.at[2]).start()
        down = jnp.zeros((hidden, kc), F32)
        for t, ph in ((0, 3), (1, 2)):
            down = down + jnp.dot(act_t[t], xin[ph, k], preferred_element_type=F32)
        wdc[k] = down.astype(BF16)
        pltpu.make_async_copy(wdc.at[k], gd.at[:, at(k, kc)], store_sem.at[3]).start()

    def early0():
        build_places()
        drain(wgu, load_sem.at[1])
        drain(wdc, load_sem.at[2])

    gain_acc[...] = jnp.zeros_like(gain_acc)
    dispatch(0, 0, 0, norm, forward_chunk, early=early0)
    forward_expert(0, 0)
    forward_return(0, 0, tokc)
    drain(cotc, load_sem.at[3])

    dispatch(2, 1, 1, cotc, backward_chunk)
    sum_b = all_sum(2, rs_b, grad_act, one_b, two_b, hidden)
    for g in range(2):
        round_into(rs_b, hidden, g)
        sum_b[0](g)

    def arrived(k, c):
        drain(hid1.at[k], z_r.at[0, k])
        return squares(hid1, k, c)

    normalize(1, hid1, lax.fori_loop(0, nk, arrived, none))
    loop(nk, lambda k: drain(yret_in.at[0, k], z_s.at[0, k]))

    def early1():
        for g in range(2):
            sum_b[1](g)
        for g in range(2):
            sum_b[2](g)
        for g in range(2):
            sum_b[3](g)

    dispatch(1, 0, 1, norm, forward_chunk, early=early1)
    forward_expert(1, 1)
    for g in range(2):
        sum_b[4](g)
    sum_b[5]()
    forward_return(1, 1, hid1)

    backward_expert(2, 1)
    backward_return(2, 1, hid1, cotc, lambda k: None)

    def arrive0(k):
        drain(grad0.at[k], z_r.at[1, k])

    dispatch(3, 1, 0, grad0, backward_chunk, arrive=arrive0)
    loop(nk, lambda k: drain(yret_in.at[1, k], z_s.at[1, k]))
    sum_b = all_sum(3, rs_b, grad_act, one_b, two_b, hidden)
    for g in range(2):
        round_into(rs_b, hidden, g)
        sum_b[0](g)
    for stage in (1, 2, 3, 4):
        for g in range(2):
            sum_b[stage](g)
    sum_b[5]()
    backward_expert(3, 0)
    backward_return(3, 0, tokc, grad0, weight_grads)

    for d in range(1, nd):
        j = lax.rem(q + d, nd)
        send(gain_acc.at[j], gain_dp.at[q], gain_s.at[0], gain_r.at[0], dp=j)
    gain_dp[q] = gain_acc[q]
    drain(gain_dp.at[0 : nd - 1], gain_r.at[0])
    mine = gain_dp[0]
    for j in range(1, nd):
        mine = mine + gain_dp[j]
    gain_ex[e] = mine
    for d in range(1, ne):
        send(gain_ex.at[e], gain_ex.at[e], gain_s.at[1], gain_r.at[1], expert=lax.rem(e + d, ne))
    drain(gain_ex.at[0 : ne - 1], gain_r.at[1])
    mine = gain_ex[0]
    for j in range(1, ne):
        mine = mine + gain_ex[j]
    gain_all[q] = mine
    for d in range(1, nd):
        send(gain_all.at[q], gain_all.at[q], gain_s.at[2], gain_r.at[2], dp=lax.rem(q + d, nd))
    drain(gain_all.at[0 : nd - 1], gain_r.at[2])
    gain_out[...] = jnp.broadcast_to(jnp.sum(gain_all[...], axis=2, keepdims=True), gain_out.shape)

    drain(gain_dp.at[0 : nd - 1], gain_s.at[0])
    drain(gain_ex.at[0 : ne - 1], gain_s.at[1])
    drain(gain_all.at[0 : nd - 1], gain_s.at[2])
    drain(dest_all.at[0 : nd - 1], dest_s)
    drain(yret_in.at[0], store_sem.at[0])
    drain(yret_in.at[1], store_sem.at[1])
    drain(wgu, store_sem.at[2])
    drain(wdc, store_sem.at[3])


def slot_rows(route_now, expert_count, dp_index, dp_count):
    tile_count = route_now.shape[0]
    order = jnp.arange(tile_count, dtype=jnp.int32)
    same = (route_now[:, None] == route_now[None, :]) & (order[None, :] < order[:, None])
    rank = jnp.sum(same.astype(jnp.int32), axis=1)
    first = (route_now * dp_count + dp_index) * (CAP * TILE) + rank * TILE
    return (first[:, None] + jnp.arange(TILE, dtype=jnp.int32)[None, :]).reshape(-1)


def body(tokens, cotangent, gain, w_gate, w_up, w_down, route):
    npipe, nd, ne = lax.axis_size("pipe"), lax.axis_size("dp"), lax.axis_size("expert")
    section = lax.axis_index("pipe")
    rows, width = tokens.shape[1:]
    quarter, hidden = w_gate.shape[2:]
    kc = min(WIDTH, quarter)
    nk = quarter // kc
    block = nd * CAP * TILE
    total = ne * block
    group = total // 2
    half = group // nd // 2
    table = route[0, :, :, 0]
    dest = []
    for t in range(PASSES):
        micro = (section - t + npipe) % npipe
        now = lax.dynamic_index_in_dim(table, micro, 0, keepdims=False)
        dest.append(slot_rows(now, ne, lax.axis_index("dp"), nd).astype(F32))
    dest = jnp.broadcast_to(jnp.stack(dest)[:, None, :], (PASSES, 8, rows))
    gain_chunks = gain[0].reshape(nd, nk, 1, kc).swapaxes(0, 1)

    hbm = pl.BlockSpec(memory_space=pl.ANY)
    vmem = pl.BlockSpec(memory_space=pltpu.VMEM)
    V = pltpu.VMEM
    S = pltpu.SemaphoreType.DMA
    chunks = (nk, nd, rows, kc)
    results = pl.pallas_call(
        functools.partial(kernel, (nd, npipe, ne, rows, width, hidden)),
        out_shape=(
            jax.ShapeDtypeStruct((rows, width), BF16),
            jax.ShapeDtypeStruct((rows, width), BF16),
            jax.ShapeDtypeStruct((nd, nk, 8, kc), F32),
            jax.ShapeDtypeStruct((quarter, hidden), BF16),
            jax.ShapeDtypeStruct((quarter, hidden), BF16),
            jax.ShapeDtypeStruct((hidden, quarter), BF16),
        ),
        in_specs=[vmem, hbm, hbm, vmem, hbm, hbm, hbm],
        out_specs=(hbm, hbm, vmem, hbm, hbm, hbm),
        scratch_shapes=[
            V(chunks, BF16),
            V(chunks, BF16),
            V(chunks, BF16),
            V(chunks, BF16),
            V(chunks, BF16),
            V((quarter, 2 * hidden), BF16),
            V((nk, hidden, kc), BF16),
            V((nd, PASSES, 8, rows), F32),
            V((PASSES, total, nd * rows), BF16),
            V((PASSES, nd * rows, total), BF16),
            V((2, nk, nd * rows, kc), BF16),
            V((nk, total, kc), BF16),
            V((4, nk, total, kc), BF16),
            V((total, 2 * hidden), F32),
            V((PASSES, total, 2 * hidden), BF16),
            V((total, hidden), BF16),
            V((PASSES, hidden, total), BF16),
            V((total, hidden), BF16),
            V((total, 2 * hidden), BF16),
            V((total, hidden), BF16),
            V((2, 2, half, 2 * hidden), BF16),
            V((2, 2, half, hidden), BF16),
            V((2, 2, 2, half, 2 * hidden), BF16),
            V((2, 2, 2, half, hidden), BF16),
            V((nk, total, kc), BF16),
            V((2, nk, total, kc), BF16),
            V((nk, nd * rows, kc), BF16),
            V((2,) + chunks, BF16),
            V((PASSES, rows, 1), F32),
            V((rows, kc), F32),
            V((nd, nk, 8, kc), F32),
            V((nd, nk, 8, kc), F32),
            V((ne, nk, 8, kc), F32),
            V((nd, nk, 8, kc), F32),
            S((4,)),
            S((4,)),
            S(()),
            S(()),
            S((4, nk)),
            S((4, nk)),
            S((4, nk)),
            S((4, nk)),
            S((4, nk)),
            S((4, nk)),
            S((4, nk)),
            S((4, nk)),
            S((2, nk)),
            S((2, nk)),
            S((4, 2, 12)),
            S((4, 2, 2)),
            S((4, 2, 2, 2)),
            S((4, 2, 3, 2)),
            S((3,)),
            S((3,)),
        ],
        compiler_params=pltpu.CompilerParams(
            collective_id=0, has_side_effects=True, vmem_limit_bytes=63_000_000
        ),
        cost_estimate=pl.CostEstimate(
            flops=36 * total * quarter * hidden, bytes_accessed=17 * 2**20, transcendentals=2 * total * hidden
        ),
    )(dest, tokens[0], cotangent[0], gain_chunks, w_gate[0, 0], w_up[0, 0], w_down[0, 0])
    out_rows, entry_grad, gain_total, grad_gate, grad_up, grad_down = results
    return (
        out_rows[None],
        entry_grad[None],
        gain_total[:, :, 0, :].reshape(1, width),
        grad_gate[None, None],
        grad_up[None, None],
        grad_down[None, None],
    )


def solution(mesh):
    placed = (
        P("pipe", ("dp", "expert"), None),
        P("pipe", ("dp", "expert"), None),
        P("pipe", None),
        P("pipe", "expert", "dp", None),
        P("pipe", "expert", "dp", None),
        P("pipe", "expert", None, "dp"),
        P("pipe", None, ("dp", "expert"), None),
    )
    return jax.shard_map(
        body,
        mesh=mesh,
        in_specs=placed,
        out_specs=(
            P("pipe", ("dp", "expert"), None),
            P("pipe", ("dp", "expert"), None),
            P("pipe", None),
            P("pipe", "expert", "dp", None),
            P("pipe", "expert", "dp", None),
            P("pipe", "expert", None, "dp"),
        ),
        check_vma=False,
    )
```

time: 723 us -> 430 us (0.59); the launches traced: 709 us -> 430 us
  Pallas kernels: 0 us -> 413 us
  waiting for transfers between devices: 312 us -> 0 us
  blocking collectives: 190 us -> 0 us
  matrix products: 98 us -> 0 us
  starting transfers between devices: 46.4 us -> 0 us
  other arithmetic: 18.6 us -> 1.78 us
  local copies, waits for them, and re-layouts: 29.4 us -> 14.5 us
  between operations: 14.4 us -> 0.72 us
    pallas_call x0 -> x1, Pallas kernels: none -> 413 us  [body(): pl.pallas_call(functools.partial(kernel, (nd, npipe, ne, rows, width, hid...]
    psum x3 -> x0, waiting for transfers between devices: 177 us -> none  [the longest x2 143 us: expert_forward(): lax.psum(up_terms.astype(jnp.bfloat16), 'dp').astype(jnp.float32)]
    psum x1 -> x0, blocking collectives: 122 us -> none  [body(): gain_total = lax.psum(gain_sum, ('dp', 'expert'))]
    dot_general x26 -> x0, matrix products: 98 us -> none  [the longest x6 30.7 us: contract_first(): lax.dot_general(former, latter, (((0,), (0,)), ((), ())), preferred_eleme...]
    all_to_all x6 -> x0, waiting for transfers between devices: 89.8 us -> none  [the longest x3 51.4 us: send_back(): lax.all_to_all(flat, ('dp', 'expert'), split_axis=0, concat_axis=0, tiled...]
    all_to_all x2 -> x0, blocking collectives: 68.4 us -> none  [the longest x1 35.5 us: send_out(): lax.all_to_all(flat, ('dp', 'expert'), split_axis=0, concat_axis=0, tiled...]
    ppermute x2 -> x0, waiting for transfers between devices: 45.3 us -> none  [shifted(): return lax.ppermute(block, axis, route)]
    all_to_all x6 -> x0, starting transfers between devices: 41.5 us -> none  [the longest x3 21.3 us: send_back(): lax.all_to_all(flat, ('dp', 'expert'), split_axis=0, concat_axis=0, tiled...]
  transfers between devices with their start and end apart: 11 -> 0, of which waited for: 11 -> 0; matrix products, arithmetic and copies ran while one was open for 9% -> 0% of each run, Pallas kernels for 0% -> 0%
where the time goes in v1:
time: 430 us
  Pallas kernels  413 us (96%)
  local copies, waits for them, and re-layouts  14.5 us (3%)
    pallas_call x1, Pallas kernels, body(): pl.pallas_call(functools.partial(kernel, (nd, npipe, ne, rows, width, hid...  413 us
    unnamed x14, local copies, waits for them, and re-layouts  10.8 us

profile of v1, /device:TPU:1, one launch (start us, length us, event | category | flops | bytes accessed | tf_op | source)
XLA Modules:
  0.0 429.9 jit_solution(16893453821964285709)
XLA Ops:
  0.7 0.7 dynamic-slice_bitcast_fusion.1
  1.3 0.2 convert_reduce_fusion
  1.6 0.1 add_convert_fusion.1
  1.6 0.1 convert_element_type.34
  1.7 0.1 add_convert_fusion
  1.8 0.1 convert_element_type.37
  1.9 0.6 broadcast_in_dim.12.dest
  2.5 0.5 broadcast.60
  3.0 1.4 reduce.3
  4.5 0.6 copy.16
  5.1 412.9 %shard_map.118 = (bf16[128,5120]{1,0:T(8,128)(2,1)}, bf16[128,5120]{1,0:T(8,128)(2,1)}, f32[4,5,8,256]{3,2,1,0:T(8,128)}, bf16[1280,768]{1,0:T(8,128)(2,1)}, bf1...) custom-call(f32[2,8,128]{2,1,0:T(8,128)} %broadcast_in_dim.12.dest, bf16[128,5120]{1,0:T(8,128)(2,1)} %bitcast.28, ...), custom_call_target="tpu_custom_call" | custom-call | flops 27179089920 | bytes 17825792 | tf_op jit(solution)/shard_map/pallas_call | solution.py:553
  418.0 0.0 copy-start.3
  418.0 1.6 slice.3
  419.6 2.5 copy.22
  422.1 0.0 copy-done.3
  422.1 0.0 copy-start.2
  422.1 1.1 copy.23
  423.2 1.0 copy-done.2
  424.1 0.0 copy-start.1
  424.1 1.3 copy.24
  425.4 1.0 copy-done.1
  426.4 0.0 copy-start
  426.4 1.3 copy.25
  427.7 1.0 copy-done
  428.6 1.3 copy.26
  (4 shorter events, 0.0 us)
Async XLA Ops:
  418.0 4.1 copy-start.3
  422.1 2.0 copy-start.2
  424.1 2.3 copy-start.1
  426.4 2.3 copy-start

commit v2 on v1

v2 whole, which is shorter than its diff:
```python
import functools
import math

import jax
import jax.numpy as jnp
from jax import lax
from jax.experimental import pallas as pl
from jax.experimental.pallas import tpu as pltpu
from jax.sharding import PartitionSpec as P

TILE = 8
CAP = 3
PASSES = 2
WIDTH = 256
epsilon = 1e-06
F32 = jnp.float32
BF16 = jnp.bfloat16


def kernel(
    sizes,
    dest, tok, cot, gain, wg, wu, wd,
    out_tok, grad_tok, gain_out, gg, gu, gd,
    tokc, cotc, hid1, grad0, norm, wgu, wdc, dest_own, dest_all, place, back,
    yin, xout, xin, acc, gate_up, act, act_t, grad_act,
    rs_f, rs_b, one_f, one_b, two_f, two_b,
    ret_out, ret_in, yret_out, yret_in, inverse, mean_acc, gain_acc, gain_dp, gain_ex, gain_all,
    load_sem, store_sem, dest_s, dest_r, y_s, y_r, x_s, x_r, rx_s, rx_r, ry_s, ry_r,
    z_s, z_r, ar_s, one_r, two_r, ag_r, gain_s, gain_r,
):
    nd, npipe, ne, rows, width, hidden = sizes
    quarter = width // nd
    kc = min(WIDTH, quarter)
    nk = quarter // kc
    block = nd * CAP * TILE
    total = ne * block
    unit = nd * TILE
    lanes = ((0, unit), (ne * unit, (CAP - 1) * unit))
    q, p, e = lax.axis_index("dp"), lax.axis_index("pipe"), lax.axis_index("expert")
    q_up, q_down, q_far = lax.rem(q + 1, nd), lax.rem(q + nd - 1, nd), lax.rem(q + 2, nd)
    p_up, p_down = lax.rem(p + 1, npipe), lax.rem(p + npipe - 1, npipe)

    def send(src, dst, ssem, rsem, **where):
        pltpu.make_async_remote_copy(
            src_ref=src, dst_ref=dst, send_sem=ssem, recv_sem=rsem,
            device_id=where, device_id_type=pl.DeviceIdType.MESH,
        ).start()

    def drain(ref, sem):
        pltpu.make_async_copy(ref, ref, sem).wait()

    def loop(count, step):
        lax.fori_loop(0, count, lambda i, c: (step(i), c)[1], 0)

    def at(i, size):
        return pl.ds(pl.multiple_of(i * size, size), size)

    def rows_of(g, i):
        base, size = lanes[g]
        return pl.ds(pl.multiple_of(base + i * size, unit), size)

    def span_of(g):
        base, size = lanes[g]
        return slice(base, base + ne * size)

    def gain_of(k, j):
        return gain[0:1, pl.ds(pl.multiple_of(j * quarter + k * kc, kc), kc)]

    for k in range(nk):
        for j in range(nd):
            cols = pl.ds(j * quarter + k * kc, kc)
            pltpu.make_async_copy(tok.at[:, cols], tokc.at[k, j], load_sem.at[0]).start()
    pltpu.make_async_copy(wg, wgu.at[:, 0:hidden], load_sem.at[1]).start()
    pltpu.make_async_copy(wu, wgu.at[:, hidden : 2 * hidden], load_sem.at[1]).start()
    for k in range(nk):
        pltpu.make_async_copy(wd.at[:, pl.ds(k * kc, kc)], wdc.at[k], load_sem.at[2]).start()
    for k in range(nk):
        for j in range(nd):
            cols = pl.ds(j * quarter + k * kc, kc)
            pltpu.make_async_copy(cot.at[:, cols], cotc.at[k, j], load_sem.at[3]).start()

    barrier = pltpu.get_barrier_semaphore()

    def greet(**where):
        pl.semaphore_signal(barrier, inc=1, device_id=where, device_id_type=pl.DeviceIdType.MESH)

    for d in range(1, nd):
        greet(dp=lax.rem(q + d, nd))
    for d in range(1, ne):
        greet(expert=lax.rem(e + d, ne))
    greet(pipe=p_up)
    greet(pipe=p_down)

    drain(tokc, load_sem.at[0])

    def squares(ref, k, before):
        for j in range(nd):
            wide = ref[k, j].astype(F32)
            before = before + jnp.sum(wide * wide, axis=-1, keepdims=True)
        return before

    def normalize(t, ref, total_squares):
        inverse[t] = lax.rsqrt(total_squares / width + epsilon)

        def step(k):
            for j in range(nd):
                norm[k, j] = (ref[k, j].astype(F32) * inverse[t] * gain_of(k, j)).astype(BF16)

        loop(nk, step)

    none = jnp.zeros((rows, 1), F32)
    normalize(0, tokc, lax.fori_loop(0, nk, lambda k, c: squares(tokc, k, c), none))
    pl.semaphore_wait(barrier, nd - 1 + ne - 1 + 2)

    row_tile = lax.broadcasted_iota(jnp.int32, (rows, rows), 1) // TILE
    row_at = lax.broadcasted_iota(jnp.int32, (1, rows), 1)
    earlier = (row_tile.T < row_tile)
    for t in range(PASSES):
        expert_of = jnp.broadcast_to(dest[t, 0:1, :], (rows, rows))
        same = jnp.where(earlier & (expert_of.T == expert_of), 1.0, 0.0).astype(F32)
        rank = jnp.sum(same, axis=0, keepdims=True) / TILE
        inner = (q * TILE + row_at % TILE).astype(F32)
        mine = dest[t, 0:1, :]
        first = mine * unit + inner
        other = ne * unit + mine * ((CAP - 1) * unit) + (rank - 1.0) * unit + inner
        dest_own[t] = jnp.broadcast_to(jnp.where(rank < 0.5, first, other), (8, rows))
    for d in range(1, nd):
        send(dest_own, dest_all.at[q], dest_s, dest_r, dp=lax.rem(q + d, nd))
    dest_all[q] = dest_own[...]

    def build_places():
        drain(dest_all.at[0 : nd - 1], dest_r)
        slot_ids = lax.broadcasted_iota(jnp.int32, (total, rows), 0).astype(F32)
        for t in range(PASSES):
            for s in range(nd):
                hot = jnp.where(slot_ids == dest_all[s, t, 0:1, :], 1.0, 0.0).astype(F32)
                place[t, :, s * rows : (s + 1) * rows] = hot.astype(BF16)
                back[t, s * rows : (s + 1) * rows, :] = hot.T.astype(BF16)


    def y_send(ph, st, src, k):
        for d in range(1, nd):
            j = lax.rem(q + d, nd)
            send(src.at[k, j], yin.at[st, k, at(q, rows)], y_s.at[ph, k], y_r.at[ph, k], dp=j)
        yin[st, k, at(q, rows), :] = src[k, q]

    def y_wait(ph, st, k):
        drain(yin.at[st, k, 0 : (nd - 1) * rows], y_r.at[ph, k])

    def x_send(ph, st, t, k, g):
        def some(m):
            there = at(m, ne * unit)
            xout[k, there, :] = jnp.dot(place[t, there, :], yin[st, k], preferred_element_type=F32).astype(BF16)

        if g == 0:
            some(0)
        else:
            lax.fori_loop(1, CAP, lambda m, c: (some(m), c)[1], 0)
        for d in range(1, ne):
            o = lax.rem(e + d, ne)
            send(xout.at[k, rows_of(g, o)], xin.at[ph, k, rows_of(g, e)], x_s.at[ph, k, g], x_r.at[ph, k, g], expert=o)
        xin[ph, k, rows_of(g, e), :] = xout[k, rows_of(g, e), :]

    def x_wait(ph, k, g):
        drain(xin.at[ph, k, 0 : (ne - 1) * lanes[g][1]], x_r.at[ph, k, g])

    def over_lane(g, step):
        base, size = lanes[g]
        first = base // (ne * unit)
        lax.fori_loop(first, first + size // unit, lambda m, c: (step(at(m, ne * unit)), c)[1], 0)

    def forward_chunk(ph, k, g):
        x_wait(ph, k, g)

        def some(there):
            acc[there, :] += jnp.dot(xin[ph, k, there, :], wgu[at(k, kc), :], preferred_element_type=F32)

        over_lane(g, some)

    def backward_chunk(ph, k, g):
        x_wait(ph, k, g)

        def some(there):
            acc[there, 0:hidden] += lax.dot_general(
                xin[ph, k, there, :], wdc[k], (((1,), (1,)), ((), ())), preferred_element_type=F32
            )

        over_lane(g, some)

    def settle_y(ph, st):
        loop(nk, lambda k: drain(yin.at[st, k, 0 : (nd - 1) * rows], y_s.at[ph, k]))

    def settle_x(ph):
        def step(k):
            for g in range(2):
                drain(xout.at[k, 0 : (ne - 1) * lanes[g][1]], x_s.at[ph, k, g])

        loop(nk, step)

    def all_sum(ph, src, dst, one, two, columns):
        def half_of(g):
            return ne * lanes[g][1] // nd // 2

        def span(g, b, h):
            half = half_of(g)
            return pl.ds(pl.multiple_of(lanes[g][0] + (2 * b + h) * half, half), half)

        def cut(ref, g):
            return ref.at[0 : half_of(g)]

        def open_(g):
            send(src.at[span(g, q_far, 0)], cut(one.at[g, 0], g), ar_s.at[ph, g, 0], one_r.at[ph, g, 0], dp=q_down)
            send(src.at[span(g, q_far, 1)], cut(one.at[g, 1], g), ar_s.at[ph, g, 1], one_r.at[ph, g, 1], dp=q_up)
            send(src.at[span(g, q_down, 1)], cut(two.at[g, 0, 1], g), ar_s.at[ph, g, 2], two_r.at[ph, g, 0, 1], dp=q_down)
            send(src.at[span(g, q_up, 0)], cut(two.at[g, 1, 0], g), ar_s.at[ph, g, 3], two_r.at[ph, g, 1, 0], dp=q_up)

        def middle(g):
            half = half_of(g)
            for side, b in ((0, q_down), (1, q_up)):
                drain(cut(one.at[g, side], g), one_r.at[ph, g, side])
                there = span(g, b, side)
                src[there, :] = (src[there, :].astype(F32) + one[g, side, 0:half].astype(F32)).astype(BF16)
                send(src.at[there], cut(two.at[g, side, side], g), ar_s.at[ph, g, 4 + side], two_r.at[ph, g, side, side], dp=b)

        def own(g):
            half = half_of(g)
            for h in range(2):
                for side in range(2):
                    drain(cut(two.at[g, side, h], g), two_r.at[ph, g, side, h])
                mine = span(g, q, h)
                dst[mine, :] = (
                    src[mine, :].astype(F32) + two[g, 0, h, 0:half].astype(F32) + two[g, 1, h, 0:half].astype(F32)
                ).astype(BF16)
            for i in range(2):
                up, down = span(g, q, i), span(g, q, 1 - i)
                send(dst.at[up], dst.at[up], ar_s.at[ph, g, 6 + i], ag_r.at[ph, g, 0, i], dp=q_up)
                send(dst.at[down], dst.at[down], ar_s.at[ph, g, 8 + i], ag_r.at[ph, g, 1, 1 - i], dp=q_down)

        def pass_on(g):
            first, second = span(g, q_down, 0), span(g, q_up, 1)
            drain(dst.at[first], ag_r.at[ph, g, 0, 0])
            send(dst.at[first], dst.at[first], ar_s.at[ph, g, 10], ag_r.at[ph, g, 2, 0], dp=q_up)
            drain(dst.at[second], ag_r.at[ph, g, 1, 1])
            send(dst.at[second], dst.at[second], ar_s.at[ph, g, 11], ag_r.at[ph, g, 2, 1], dp=q_down)

        def close(g):
            drain(dst.at[span(g, q_down, 1)], ag_r.at[ph, g, 0, 1])
            drain(dst.at[span(g, q_up, 0)], ag_r.at[ph, g, 1, 0])
            drain(dst.at[span(g, q_far, 0)], ag_r.at[ph, g, 2, 0])
            drain(dst.at[span(g, q_far, 1)], ag_r.at[ph, g, 2, 1])

        def settle(g):
            for i in range(12):
                drain(cut(src, g), ar_s.at[ph, g, i])

        return open_, middle, own, pass_on, close, settle

    def small_steps(g, step):
        size = math.gcd(64, ne * unit)
        base, length = lanes[g]
        first = base // size
        lax.fori_loop(first, first + ne * length // size, lambda m, c: (step(at(m, size)), c)[1], 0)

    def round_into(src, columns, g):
        def some(there):
            src[there, :] = acc[there, 0:columns].astype(BF16)

        small_steps(g, some)

    def ret_send(ph, st, g, k):
        for d in range(1, ne):
            o = lax.rem(e + d, ne)
            send(
                ret_out.at[k, rows_of(g, o)], ret_in.at[st, k, rows_of(g, e)],
                rx_s.at[ph, k, g], rx_r.at[ph, k, g], expert=o,
            )
        ret_in[st, k, rows_of(g, e), :] = ret_out[k, rows_of(g, e), :]

    def settle_ret(ph, g):
        loop(nk, lambda k: drain(ret_out.at[k, 0 : (ne - 1) * lanes[g][1]], rx_s.at[ph, k, g]))

    def settle_yret(ph):
        loop(nk, lambda k: drain(yret_out.at[k, 0 : (nd - 1) * rows], ry_s.at[ph, k]))

    short = nd * rows // 2

    def collect(ph, st, t, k):
        for g in range(2):
            drain(ret_in.at[st, k, 0 : (ne - 1) * lanes[g][1]], rx_r.at[ph, k, g])

        def some(m):
            yret_out[k, at(m, short), :] = jnp.dot(
                back[t, at(m, short), :], ret_in[st, k], preferred_element_type=F32
            ).astype(BF16)

        loop(2, some)
        for d in range(1, nd):
            j = lax.rem(q + d, nd)
            send(yret_out.at[k, at(j, rows)], yret_in.at[st, k, q], ry_s.at[ph, k], ry_r.at[ph, k], dp=j)
        yret_in[st, k, q] = yret_out[k, at(q, rows), :]

    def landed(ph, st, k):
        drain(yret_in.at[st, k, 0 : nd - 1], ry_r.at[ph, k])

    def activate(t, g):
        def some(there):
            gate = gate_up[t, there, 0:hidden].astype(F32)
            up = gate_up[t, there, hidden : 2 * hidden].astype(F32)
            act[there, :] = (gate * jax.nn.sigmoid(gate) * up).astype(BF16)

        small_steps(g, some)

    def forward_down(ph, g):
        mine = span_of(g)

        def down(k):
            ret_out[k, mine, :] = jnp.dot(act[mine, :], wdc[k], preferred_element_type=F32).astype(BF16)
            ret_send(ph, 0, g, k)

        loop(nk, down)

    def turn(t):
        wide = math.gcd(total, 128)
        for m in range(total // wide):
            act_t[t, :, m * wide : (m + 1) * wide] = act[m * wide : (m + 1) * wide, :].T

    def before(t, g, with_act):
        def some(there):
            gate = gate_up[t, there, 0:hidden].astype(F32)
            up = gate_up[t, there, hidden : 2 * hidden].astype(F32)
            grad = grad_act[there, :].astype(F32)
            s = jax.nn.sigmoid(gate)
            silu = gate * s
            if with_act:
                act[there, :] = (silu * up).astype(BF16)
            gate_up[t, there, 0:hidden] = (grad * up * s * (1.0 + gate * (1.0 - s))).astype(BF16)
            gate_up[t, there, hidden : 2 * hidden] = (grad * silu).astype(BF16)

        small_steps(g, some)

    def backward_up(ph, t, g):
        mine = span_of(g)

        def up_(k):
            ret_out[k, mine, :] = lax.dot_general(
                gate_up[t, mine, :], wgu[at(k, kc), :], (((1,), (1,)), ((), ())), preferred_element_type=F32
            ).astype(BF16)
            ret_send(ph, 1, g, k)

        loop(nk, up_)

    def to_rows(ref, k, out, sem):
        for j in range(nd):
            cols = pl.ds(pl.multiple_of(j * quarter + k * kc, kc), kc)
            pltpu.make_async_copy(ref.at[k, j], out.at[:, cols], sem).start()

    def add_rows(ph, ref, k):
        landed(ph, 0, k)
        for j in range(nd):
            yret_in[0, k, j] = (ref[k, j].astype(F32) + yret_in[0, k, j].astype(F32)).astype(BF16)

    def terms(t, ref, k, j):
        return yret_in[1, k, j].astype(F32), ref[k, j].astype(F32) * inverse[t]

    def gather_grads(ph, t, ref, k):
        landed(ph, 1, k)
        fresh = mean_acc[...]
        for j in range(nd):
            u, scaled = terms(t, ref, k, j)
            both = u * scaled
            gain_acc[j, k] += jnp.sum(both.reshape(rows // 8, 8, kc), axis=0)
            fresh = fresh + both * gain_of(k, j)
        mean_acc[...] = fresh

    def finish_grads(t, ref, grad_ref, k, mean):
        for j in range(nd):
            u, scaled = terms(t, ref, k, j)
            wide = inverse[t] * (u * gain_of(k, j) - scaled * mean)
            yret_in[1, k, j] = (grad_ref[k, j].astype(F32) + wide).astype(BF16)

    def mean_of():
        return jnp.sum(mean_acc[...], axis=-1, keepdims=True) / width

    def weight_grads(k):
        both = jnp.zeros((kc, 2 * hidden), F32)
        for t in range(PASSES):
            both = both + lax.dot_general(
                xin[t, k], gate_up[t], (((0,), (0,)), ((), ())), preferred_element_type=F32
            )
        wgu[at(k, kc), :] = both.astype(BF16)
        pltpu.make_async_copy(wgu.at[at(k, kc), 0:hidden], gg.at[at(k, kc)], store_sem.at[2]).start()
        pltpu.make_async_copy(wgu.at[at(k, kc), hidden : 2 * hidden], gu.at[at(k, kc)], store_sem.at[2]).start()
        down = jnp.zeros((hidden, kc), F32)
        for t, ph in ((0, 3), (1, 2)):
            down = down + jnp.dot(act_t[t], xin[ph, k], preferred_element_type=F32)
        wdc[k] = down.astype(BF16)
        pltpu.make_async_copy(wdc.at[k], gd.at[:, at(k, kc)], store_sem.at[3]).start()

    lag = 2

    def when(test, step):
        @pl.when(test)
        def _():
            step()

    def forward_to_sums(ph, st, t, sums):
        open_, middle, own, pass_on, close, settle = sums
        acc[...] = jnp.zeros_like(acc)

        def step(i):
            def first():
                y_wait(ph, st, i)
                x_send(ph, st, t, i, 0)

            when(i < nk, first)
            when(i >= lag, lambda: x_send(ph, st, t, i - lag, 1))
            when(i >= 1, lambda: forward_chunk(ph, i - 1, 0))
            when(i >= lag + 1, lambda: forward_chunk(ph, i - lag - 1, 1))

        loop(nk + 1, step)
        round_into(rs_f, 2 * hidden, 0)
        open_(0)
        for k in range(nk + 1 - lag, nk):
            x_send(ph, st, t, k, 1)
        for n, k in enumerate(range(nk - lag, nk)):
            forward_chunk(ph, k, 1)
            if n == 0:
                middle(0)
        own(0)
        round_into(rs_f, 2 * hidden, 1)
        open_(1)
        pass_on(0)
        middle(1)

    gain_acc[...] = jnp.zeros_like(gain_acc)
    loop(nk, lambda k: y_send(0, 0, norm, k))
    build_places()
    drain(wgu, load_sem.at[1])
    drain(wdc, load_sem.at[2])
    drain(cotc, load_sem.at[3])

    sums = all_sum(0, rs_f, gate_up.at[0], one_f, two_f, 2 * hidden)
    forward_to_sums(0, 0, 0, sums)
    sums[4](0)
    activate(0, 0)
    forward_down(0, 0)
    sums[2](1)
    sums[3](1)
    settle_y(0, 0)
    settle_x(0)
    sums[4](1)
    activate(0, 1)
    forward_down(0, 1)
    acc[:, 0:hidden] = jnp.zeros((total, hidden), F32)

    def turn_round(i):
        def first():
            collect(0, 0, 0, i)
            y_send(2, 1, cotc, i)

        def second():
            k = i - 1
            add_rows(0, tokc, k)
            send(yret_in.at[0, k], hid1.at[k], z_s.at[0, k], z_r.at[0, k], pipe=p_up)
            y_wait(2, 1, k)
            x_send(2, 1, 1, k, 0)
            x_send(2, 1, 1, k, 1)

        def third():
            backward_chunk(2, i - 2, 0)
            backward_chunk(2, i - 2, 1)

        when(i < nk, first)
        when((i >= 1) & (i <= nk), second)
        when(i >= 2, third)

    loop(nk + 2, turn_round)
    sums[5](0)
    sums[5](1)
    sums_b = all_sum(2, rs_b, grad_act, one_b, two_b, hidden)
    for g in range(2):
        round_into(rs_b, hidden, g)
        sums_b[0](g)
    turn(0)
    settle_ret(0, 0)
    settle_ret(0, 1)
    settle_yret(0)
    settle_y(2, 1)
    settle_x(2)
    for g in range(2):
        sums_b[1](g)

    def arrived(k, c):
        drain(hid1.at[k], z_r.at[0, k])
        return squares(hid1, k, c)

    so_far = lax.fori_loop(0, nk - 1, arrived, none)
    for g in range(2):
        sums_b[2](g)
    normalize(1, hid1, arrived(nk - 1, so_far))
    loop(nk, lambda k: drain(yret_in.at[0, k], z_s.at[0, k]))

    loop(nk, lambda k: y_send(1, 0, norm, k))
    for g in range(2):
        sums_b[3](g)
    for g in range(2):
        sums_b[4](g)
    sums = all_sum(1, rs_f, gate_up.at[1], one_f, two_f, 2 * hidden)
    forward_to_sums(1, 0, 1, sums)

    sums[4](0)
    sums[5](0)
    before(1, 0, True)
    backward_up(2, 1, 0)
    sums[2](1)
    sums[3](1)
    settle_y(1, 0)
    settle_x(1)
    sums_b[5](0)
    sums_b[5](1)
    sums[4](1)
    sums[5](1)
    before(1, 1, True)
    backward_up(2, 1, 1)
    mean_acc[...] = jnp.zeros_like(mean_acc)

    def back1(i):
        when(i < nk, lambda: collect(2, 1, 1, i))
        when(i >= 1, lambda: gather_grads(2, 1, hid1, i - 1))

    loop(nk + 1, back1)
    mean = mean_of()

    def leave(k):
        finish_grads(1, hid1, cotc, k, mean)
        send(yret_in.at[1, k], grad0.at[k], z_s.at[1, k], z_r.at[1, k], pipe=p_down)

    loop(nk, leave)
    settle_ret(2, 0)
    settle_ret(2, 1)
    settle_yret(2)

    forward_down(1, 0)
    acc[:, 0:hidden] = jnp.zeros((total, hidden), F32)

    def come(i):
        def first():
            drain(grad0.at[i], z_r.at[1, i])
            y_send(3, 1, grad0, i)

        def second():
            y_wait(3, 1, i - 1)
            x_send(3, 1, 0, i - 1, 0)
            x_send(3, 1, 0, i - 1, 1)

        def third():
            backward_chunk(3, i - 2, 0)
            backward_chunk(3, i - 2, 1)

        when(i < nk, first)
        when((i >= 1) & (i <= nk), second)
        when(i >= 2, third)

    loop(nk + 2, come)
    loop(nk, lambda k: drain(yret_in.at[1, k], z_s.at[1, k]))
    sums_b = all_sum(3, rs_b, grad_act, one_b, two_b, hidden)
    for g in range(2):
        round_into(rs_b, hidden, g)
        sums_b[0](g)
    forward_down(1, 1)
    for g in range(2):
        sums_b[1](g)
    sums_b[2](0)
    sums_b[2](1)
    turn(1)
    sums_b[3](0)
    sums_b[3](1)
    settle_ret(1, 0)
    sums_b[4](0)
    before(0, 0, False)
    backward_up(3, 0, 0)
    settle_ret(1, 1)
    sums_b[4](1)
    before(0, 1, False)
    backward_up(3, 0, 1)
    settle_y(3, 1)
    settle_x(3)

    def leave1(i):
        when(i < nk, lambda: collect(1, 0, 1, i))

        def second():
            add_rows(1, hid1, i - 1)
            to_rows(yret_in.at[0], i - 1, out_tok, store_sem.at[0])

        when(i >= 1, second)

    loop(nk + 1, leave1)
    settle_yret(1)
    mean_acc[...] = jnp.zeros_like(mean_acc)

    def back0(i):
        when(i < nk, lambda: collect(3, 1, 0, i))
        when(i >= 1, lambda: gather_grads(3, 0, tokc, i - 1))
        when(i < nk - 1, lambda: weight_grads(i))

    loop(nk + 1, back0)
    for d in range(1, nd):
        j = lax.rem(q + d, nd)
        send(gain_acc.at[j], gain_dp.at[q], gain_s.at[0], gain_r.at[0], dp=j)
    mean = mean_of()

    def last(k):
        finish_grads(0, tokc, grad0, k, mean)
        to_rows(yret_in.at[1], k, grad_tok, store_sem.at[1])

    loop(nk, last)

    gain_dp[q] = gain_acc[q]
    drain(gain_dp.at[0 : nd - 1], gain_r.at[0])
    mine = gain_dp[0]
    for j in range(1, nd):
        mine = mine + gain_dp[j]
    gain_ex[e] = mine
    for d in range(1, ne):
        send(gain_ex.at[e], gain_ex.at[e], gain_s.at[1], gain_r.at[1], expert=lax.rem(e + d, ne))
    weight_grads(nk - 1)
    drain(gain_ex.at[0 : ne - 1], gain_r.at[1])
    mine = gain_ex[0]
    for j in range(1, ne):
        mine = mine + gain_ex[j]
    gain_all[q] = mine
    for d in range(1, nd):
        send(gain_all.at[q], gain_all.at[q], gain_s.at[2], gain_r.at[2], dp=lax.rem(q + d, nd))
    drain(gain_all.at[0 : nd - 1], gain_r.at[2])
    gain_out[...] = jnp.broadcast_to(jnp.sum(gain_all[...], axis=2, keepdims=True), gain_out.shape)

    sums_b[5](0)
    sums_b[5](1)
    settle_ret(3, 0)
    settle_ret(3, 1)
    settle_yret(3)
    drain(gain_dp.at[0 : nd - 1], gain_s.at[0])
    drain(gain_ex.at[0 : ne - 1], gain_s.at[1])
    drain(gain_all.at[0 : nd - 1], gain_s.at[2])
    drain(dest_all.at[0 : nd - 1], dest_s)
    drain(yret_in.at[0], store_sem.at[0])
    drain(yret_in.at[1], store_sem.at[1])
    drain(wgu, store_sem.at[2])
    drain(wdc, store_sem.at[3])


def hand_over(quarter, kc, *refs):
    got, given, sems = refs[0:6], refs[6:12], refs[12]
    copies = []
    for n, i in enumerate((3, 4, 5, 0, 1)):
        size = got[i].shape[0] // 2
        for h in range(2):
            part = pl.ds(h * size, size)
            copies.append(pltpu.make_async_copy(got[i].at[part], given[i].at[part], sems.at[n, h]))
            copies[-1].start()
    for j in range(got[2].shape[0]):
        for k in range(got[2].shape[1]):
            given[2][0:1, j * quarter + k * kc : j * quarter + (k + 1) * kc] = got[2][j, k, 0:1, :]
    for copy in copies:
        copy.wait()


def body(tokens, cotangent, gain, w_gate, w_up, w_down, route):
    npipe, nd, ne = lax.axis_size("pipe"), lax.axis_size("dp"), lax.axis_size("expert")
    section = lax.axis_index("pipe")
    rows, width = tokens.shape[1:]
    quarter, hidden = w_gate.shape[2:]
    kc = min(WIDTH, quarter)
    nk = quarter // kc
    block = nd * CAP * TILE
    total = ne * block
    half = (CAP - 1) * total // CAP // nd // 2
    table = route[0, :, :, 0]
    dest = []
    for t in range(PASSES):
        micro = (section - t + npipe) % npipe
        now = lax.dynamic_index_in_dim(table, micro, 0, keepdims=False)
        dest.append(now.astype(F32))
    dest = jnp.broadcast_to(jnp.stack(dest)[:, None, :, None], (PASSES, 8, rows // TILE, TILE))
    dest = dest.reshape(PASSES, 8, rows)

    hbm = pl.BlockSpec(memory_space=pl.ANY)
    vmem = pl.BlockSpec(memory_space=pltpu.VMEM)
    V = pltpu.VMEM
    S = pltpu.SemaphoreType.DMA
    chunks = (nk, nd, rows, kc)
    results = pl.pallas_call(
        functools.partial(kernel, (nd, npipe, ne, rows, width, hidden)),
        out_shape=(
            jax.ShapeDtypeStruct((rows, width), BF16),
            jax.ShapeDtypeStruct((rows, width), BF16),
            jax.ShapeDtypeStruct((nd, nk, 8, kc), F32),
            jax.ShapeDtypeStruct((quarter, hidden), BF16),
            jax.ShapeDtypeStruct((quarter, hidden), BF16),
            jax.ShapeDtypeStruct((hidden, quarter), BF16),
        ),
        in_specs=[vmem, hbm, hbm, vmem, hbm, hbm, hbm],
        out_specs=(hbm, hbm, vmem, hbm, hbm, hbm),
        scratch_shapes=[
            V(chunks, BF16),
            V(chunks, BF16),
            V(chunks, BF16),
            V(chunks, BF16),
            V(chunks, BF16),
            V((quarter, 2 * hidden), BF16),
            V((nk, hidden, kc), BF16),
            V((PASSES, 8, rows), F32),
            V((nd, PASSES, 8, rows), F32),
            V((PASSES, total, nd * rows), BF16),
            V((PASSES, nd * rows, total), BF16),
            V((2, nk, nd * rows, kc), BF16),
            V((nk, total, kc), BF16),
            V((4, nk, total, kc), BF16),
            V((total, 2 * hidden), F32),
            V((PASSES, total, 2 * hidden), BF16),
            V((total, hidden), BF16),
            V((PASSES, hidden, total), BF16),
            V((total, hidden), BF16),
            V((total, 2 * hidden), BF16),
            V((total, hidden), BF16),
            V((2, 2, half, 2 * hidden), BF16),
            V((2, 2, half, hidden), BF16),
            V((2, 2, 2, half, 2 * hidden), BF16),
            V((2, 2, 2, half, hidden), BF16),
            V((nk, total, kc), BF16),
            V((2, nk, total, kc), BF16),
            V((nk, nd * rows, kc), BF16),
            V((2,) + chunks, BF16),
            V((PASSES, rows, 1), F32),
            V((rows, kc), F32),
            V((nd, nk, 8, kc), F32),
            V((nd, nk, 8, kc), F32),
            V((ne, nk, 8, kc), F32),
            V((nd, nk, 8, kc), F32),
            S((4,)),
            S((4,)),
            S(()),
            S(()),
            S((4, nk)),
            S((4, nk)),
            S((4, nk, 2)),
            S((4, nk, 2)),
            S((4, nk, 2)),
            S((4, nk, 2)),
            S((4, nk)),
            S((4, nk)),
            S((2, nk)),
            S((2, nk)),
            S((4, 2, 12)),
            S((4, 2, 2)),
            S((4, 2, 2, 2)),
            S((4, 2, 3, 2)),
            S((3,)),
            S((3,)),
        ],
        compiler_params=pltpu.CompilerParams(
            collective_id=0, has_side_effects=True, vmem_limit_bytes=63_000_000
        ),
        cost_estimate=pl.CostEstimate(
            flops=36 * total * quarter * hidden, bytes_accessed=17 * 2**20, transcendentals=2 * total * hidden
        ),
    )(dest, tokens[0], cotangent[0], gain, w_gate[0, 0], w_up[0, 0], w_down[0, 0])
    out_rows, entry_grad, gain_total, grad_gate, grad_up, grad_down = pl.pallas_call(
        functools.partial(hand_over, quarter, kc),
        out_shape=(
            results[0],
            results[1],
            jax.ShapeDtypeStruct((1, width), F32),
            results[3],
            results[4],
            results[5],
        ),
        in_specs=[hbm, hbm, vmem, hbm, hbm, hbm],
        out_specs=(hbm, hbm, vmem, hbm, hbm, hbm),
        scratch_shapes=[S((5, 2))],
    )(*results)
    return (
        out_rows[None],
        entry_grad[None],
        gain_total,
        grad_gate[None, None],
        grad_up[None, None],
        grad_down[None, None],
    )


def solution(mesh):
    placed = (
        P("pipe", ("dp", "expert"), None),
        P("pipe", ("dp", "expert"), None),
        P("pipe", None),
        P("pipe", "expert", "dp", None),
        P("pipe", "expert", "dp", None),
        P("pipe", "expert", None, "dp"),
        P("pipe", None, ("dp", "expert"), None),
    )
    return jax.shard_map(
        body,
        mesh=mesh,
        in_specs=placed,
        out_specs=(
            P("pipe", ("dp", "expert"), None),
            P("pipe", ("dp", "expert"), None),
            P("pipe", None),
            P("pipe", "expert", "dp", None),
            P("pipe", "expert", "dp", None),
            P("pipe", "expert", None, "dp"),
        ),
        check_vma=False,
    )
```

time: 430 us -> 643 us (1.50)
  Pallas kernels: 413 us -> 640 us
  local copies, waits for them, and re-layouts: 14.5 us -> 0.77 us
    pallas_call x0 -> x1, Pallas kernels: none -> 261 us  [body(): pl.pallas_call(functools.partial(hand_over, quarter, kc), out_shape=(resu...]
    pallas_call x1, Pallas kernels: 413 us -> 380 us  [body(): pl.pallas_call(functools.partial(kernel, (nd, npipe, ne, rows, width, hid...]
    unnamed x14 -> x0, local copies, waits for them, and re-layouts: 10.8 us -> none
where the time goes in v2:
time: 643 us
  Pallas kernels  640 us (100%)
    pallas_call x1, Pallas kernels, body(): pl.pallas_call(functools.partial(kernel, (nd, npipe, ne, rows, width, hid...  380 us
    pallas_call x1, Pallas kernels, body(): pl.pallas_call(functools.partial(hand_over, quarter, kc), out_shape=(resu...  261 us

profile of v2, /device:TPU:1, one launch (start us, length us, event | category | flops | bytes accessed | tf_op | source)
XLA Modules:
  0.0 642.7 jit_solution(9196304568113635782)
XLA Ops:
  0.7 0.7 convert_bitcast_fusion.1
  1.4 0.1 broadcast_in_dim.25
  1.4 0.1 broadcast_in_dim.26
  1.5 0.6 broadcast_in_dim.27.dest
  2.1 379.6 %shard_map.118 = (bf16[128,5120]{1,0:T(8,128)(2,1)}, bf16[128,5120]{1,0:T(8,128)(2,1)}, f32[4,5,8,256]{3,2,1,0:T(8,128)}, bf16[1280,768]{1,0:T(8,128)(2,1)}, bf1...) custom-call(f32[2,8,128]{2,1,0:T(8,128)} %broadcast_in_dim.27.dest, bf16[128,5120]{1,0:T(8,128)(2,1)} %bitcast.20, ...), custom_call_target="tpu_custom_call" | custom-call | flops 27179089920 | bytes 17825792 | tf_op jit(solution)/shard_map/pallas_call | solution.py:693
  381.7 260.8 %shard_map.119 = (bf16[128,5120]{1,0:T(8,128)(2,1)}, bf16[128,5120]{1,0:T(8,128)(2,1)}, f32[1,5120]{1,0:T(1,128)}, bf16[1280,768]{1,0:T(8,128)(2,1)}, bf16[1280,...) custom-call(bf16[128,5120]{1,0:T(8,128)(2,1)} %get-tuple-element.18.refs_0_, bf16[128,5120]{1,0:T(8,128)(2,1)} %get-tuple-element.19.refs_1_, ...), custom_call_target="tpu_custom_call" | custom-call | tf_op jit(solution)/shard_map/pallas_call | solution.py:769
  (1 shorter events, 0.0 us)

commit v3 on v2

--- a/solution.py
+++ b/solution.py
@@ -26,7 +26,7 @@
     rs_f, rs_b, one_f, one_b, two_f, two_b,
     ret_out, ret_in, yret_out, yret_in, inverse, mean_acc, gain_acc, gain_dp, gain_ex, gain_all,
     load_sem, store_sem, dest_s, dest_r, y_s, y_r, x_s, x_r, rx_s, rx_r, ry_s, ry_r,
-    z_s, z_r, ar_s, one_r, two_r, ag_r, gain_s, gain_r,
+    z_s, z_r, sum_s, one_r, two_r, give_s, give_r, gain_s, gain_r,
 ):
     nd, npipe, ne, rows, width, hidden = sizes
     quarter = width // nd
@@ -35,7 +35,9 @@
     block = nd * CAP * TILE
     total = ne * block
     unit = nd * TILE
-    lanes = ((0, unit), (ne * unit, (CAP - 1) * unit))
+    lane = ne * unit
+    lanes = range(CAP)
+    half = lane // nd // 2
     q, p, e = lax.axis_index("dp"), lax.axis_index("pipe"), lax.axis_index("expert")
     q_up, q_down, q_far = lax.rem(q + 1, nd), lax.rem(q + nd - 1, nd), lax.rem(q + 2, nd)
     p_up, p_down = lax.rem(p + 1, npipe), lax.rem(p + npipe - 1, npipe)
@@ -56,12 +58,10 @@
         return pl.ds(pl.multiple_of(i * size, size), size)
 
     def rows_of(g, i):
-        base, size = lanes[g]
-        return pl.ds(pl.multiple_of(base + i * size, unit), size)
+        return pl.ds(pl.multiple_of(g * lane + i * unit, unit), unit)
 
     def span_of(g):
-        base, size = lanes[g]
-        return slice(base, base + ne * size)
+        return slice(g * lane, (g + 1) * lane)
 
     def gain_of(k, j):
         return gain[0:1, pl.ds(pl.multiple_of(j * quarter + k * kc, kc), kc)]
@@ -121,9 +121,7 @@
         rank = jnp.sum(same, axis=0, keepdims=True) / TILE
         inner = (q * TILE + row_at % TILE).astype(F32)
         mine = dest[t, 0:1, :]
-        first = mine * unit + inner
-        other = ne * unit + mine * ((CAP - 1) * unit) + (rank - 1.0) * unit + inner
-        dest_own[t] = jnp.broadcast_to(jnp.where(rank < 0.5, first, other), (8, rows))
+        dest_own[t] = jnp.broadcast_to(rank * lane + mine * unit + inner, (8, rows))
     for d in range(1, nd):
         send(dest_own, dest_all.at[q], dest_s, dest_r, dp=lax.rem(q + d, nd))
     dest_all[q] = dest_own[...]
@@ -148,118 +146,100 @@
         drain(yin.at[st, k, 0 : (nd - 1) * rows], y_r.at[ph, k])
 
     def x_send(ph, st, t, k, g):
-        def some(m):
-            there = at(m, ne * unit)
-            xout[k, there, :] = jnp.dot(place[t, there, :], yin[st, k], preferred_element_type=F32).astype(BF16)
-
-        if g == 0:
-            some(0)
-        else:
-            lax.fori_loop(1, CAP, lambda m, c: (some(m), c)[1], 0)
+        mine = span_of(g)
+        xout[k, mine, :] = jnp.dot(place[t, mine, :], yin[st, k], preferred_element_type=F32).astype(BF16)
         for d in range(1, ne):
             o = lax.rem(e + d, ne)
             send(xout.at[k, rows_of(g, o)], xin.at[ph, k, rows_of(g, e)], x_s.at[ph, k, g], x_r.at[ph, k, g], expert=o)
         xin[ph, k, rows_of(g, e), :] = xout[k, rows_of(g, e), :]
 
     def x_wait(ph, k, g):
-        drain(xin.at[ph, k, 0 : (ne - 1) * lanes[g][1]], x_r.at[ph, k, g])
-
-    def over_lane(g, step):
-        base, size = lanes[g]
-        first = base // (ne * unit)
-        lax.fori_loop(first, first + size // unit, lambda m, c: (step(at(m, ne * unit)), c)[1], 0)
+        drain(xin.at[ph, k, 0 : (ne - 1) * unit], x_r.at[ph, k, g])
 
     def forward_chunk(ph, k, g):
         x_wait(ph, k, g)
-
-        def some(there):
-            acc[there, :] += jnp.dot(xin[ph, k, there, :], wgu[at(k, kc), :], preferred_element_type=F32)
-
-        over_lane(g, some)
-
-    def backward_chunk(ph, k, g):
-        x_wait(ph, k, g)
-
-        def some(there):
+        mine = span_of(g)
+        acc[mine, :] += jnp.dot(xin[ph, k, mine, :], wgu[at(k, kc), :], preferred_element_type=F32)
+
+    def backward_chunk(ph, k):
+        for g in lanes:
+            x_wait(ph, k, g)
+
+        def some(m):
+            there = at(m, lane)
             acc[there, 0:hidden] += lax.dot_general(
                 xin[ph, k, there, :], wdc[k], (((1,), (1,)), ((), ())), preferred_element_type=F32
             )
 
-        over_lane(g, some)
+        loop(CAP, some)
 
     def settle_y(ph, st):
         loop(nk, lambda k: drain(yin.at[st, k, 0 : (nd - 1) * rows], y_s.at[ph, k]))
 
     def settle_x(ph):
         def step(k):
-            for g in range(2):
-                drain(xout.at[k, 0 : (ne - 1) * lanes[g][1]], x_s.at[ph, k, g])
+            for g in lanes:
+                drain(xout.at[k, 0 : (ne - 1) * unit], x_s.at[ph, k, g])
 
         loop(nk, step)
 
-    def all_sum(ph, src, dst, one, two, columns):
-        def half_of(g):
-            return ne * lanes[g][1] // nd // 2
-
-        def span(g, b, h):
-            half = half_of(g)
-            return pl.ds(pl.multiple_of(lanes[g][0] + (2 * b + h) * half, half), half)
-
-        def cut(ref, g):
-            return ref.at[0 : half_of(g)]
-
+    def span(g, b, h):
+        return pl.ds(pl.multiple_of(g * lane + (2 * b + h) * half, half), half)
+
+    def summing(ph, src, one, two):
         def open_(g):
-            send(src.at[span(g, q_far, 0)], cut(one.at[g, 0], g), ar_s.at[ph, g, 0], one_r.at[ph, g, 0], dp=q_down)
-            send(src.at[span(g, q_far, 1)], cut(one.at[g, 1], g), ar_s.at[ph, g, 1], one_r.at[ph, g, 1], dp=q_up)
-            send(src.at[span(g, q_down, 1)], cut(two.at[g, 0, 1], g), ar_s.at[ph, g, 2], two_r.at[ph, g, 0, 1], dp=q_down)
-            send(src.at[span(g, q_up, 0)], cut(two.at[g, 1, 0], g), ar_s.at[ph, g, 3], two_r.at[ph, g, 1, 0], dp=q_up)
+            send(src.at[span(g, q_far, 0)], one.at[g, 0], sum_s.at[ph, g, 0], one_r.at[ph, g, 0], dp=q_down)
+            send(src.at[span(g, q_far, 1)], one.at[g, 1], sum_s.at[ph, g, 1], one_r.at[ph, g, 1], dp=q_up)
+            send(src.at[span(g, q_down, 1)], two.at[g, 0, 1], sum_s.at[ph, g, 2], two_r.at[ph, g, 0, 1], dp=q_down)
+            send(src.at[span(g, q_up, 0)], two.at[g, 1, 0], sum_s.at[ph, g, 3], two_r.at[ph, g, 1, 0], dp=q_up)
 
         def middle(g):
-            half = half_of(g)
             for side, b in ((0, q_down), (1, q_up)):
-                drain(cut(one.at[g, side], g), one_r.at[ph, g, side])
+                drain(one.at[g, side], one_r.at[ph, g, side])
                 there = span(g, b, side)
-                src[there, :] = (src[there, :].astype(F32) + one[g, side, 0:half].astype(F32)).astype(BF16)
-                send(src.at[there], cut(two.at[g, side, side], g), ar_s.at[ph, g, 4 + side], two_r.at[ph, g, side, side], dp=b)
-
-        def own(g):
-            half = half_of(g)
-            for h in range(2):
-                for side in range(2):
-                    drain(cut(two.at[g, side, h], g), two_r.at[ph, g, side, h])
-                mine = span(g, q, h)
-                dst[mine, :] = (
-                    src[mine, :].astype(F32) + two[g, 0, h, 0:half].astype(F32) + two[g, 1, h, 0:half].astype(F32)
-                ).astype(BF16)
+                src[there, :] = (src[there, :].astype(F32) + one[g, side].astype(F32)).astype(BF16)
+                send(src.at[there], two.at[g, side, side], sum_s.at[ph, g, 4 + side], two_r.at[ph, g, side, side], dp=b)
+
+        def whole(g, h):
+            for side in range(2):
+                drain(two.at[g, side, h], two_r.at[ph, g, side, h])
+            return src[span(g, q, h), :].astype(F32) + two[g, 0, h].astype(F32) + two[g, 1, h].astype(F32)
+
+        def settle(g):
+            for i in range(6):
+                drain(src.at[0:half], sum_s.at[ph, g, i])
+
+        return open_, middle, whole, settle
+
+    def giving(ph, dst):
+        def offer(g):
             for i in range(2):
                 up, down = span(g, q, i), span(g, q, 1 - i)
-                send(dst.at[up], dst.at[up], ar_s.at[ph, g, 6 + i], ag_r.at[ph, g, 0, i], dp=q_up)
-                send(dst.at[down], dst.at[down], ar_s.at[ph, g, 8 + i], ag_r.at[ph, g, 1, 1 - i], dp=q_down)
+                send(dst.at[up], dst.at[up], give_s.at[ph, g, i], give_r.at[ph, g, 0, i], dp=q_up)
+                send(dst.at[down], dst.at[down], give_s.at[ph, g, 2 + i], give_r.at[ph, g, 1, 1 - i], dp=q_down)
 
         def pass_on(g):
             first, second = span(g, q_down, 0), span(g, q_up, 1)
-            drain(dst.at[first], ag_r.at[ph, g, 0, 0])
-            send(dst.at[first], dst.at[first], ar_s.at[ph, g, 10], ag_r.at[ph, g, 2, 0], dp=q_up)
-            drain(dst.at[second], ag_r.at[ph, g, 1, 1])
-            send(dst.at[second], dst.at[second], ar_s.at[ph, g, 11], ag_r.at[ph, g, 2, 1], dp=q_down)
+            drain(dst.at[first], give_r.at[ph, g, 0, 0])
+            send(dst.at[first], dst.at[first], give_s.at[ph, g, 4], give_r.at[ph, g, 2, 0], dp=q_up)
+            drain(dst.at[second], give_r.at[ph, g, 1, 1])
+            send(dst.at[second], dst.at[second], give_s.at[ph, g, 5], give_r.at[ph, g, 2, 1], dp=q_down)
 
         def close(g):
-            drain(dst.at[span(g, q_down, 1)], ag_r.at[ph, g, 0, 1])
-            drain(dst.at[span(g, q_up, 0)], ag_r.at[ph, g, 1, 0])
-            drain(dst.at[span(g, q_far, 0)], ag_r.at[ph, g, 2, 0])
-            drain(dst.at[span(g, q_far, 1)], ag_r.at[ph, g, 2, 1])
+            drain(dst.at[span(g, q_down, 1)], give_r.at[ph, g, 0, 1])
+            drain(dst.at[span(g, q_up, 0)], give_r.at[ph, g, 1, 0])
+            drain(dst.at[span(g, q_far, 0)], give_r.at[ph, g, 2, 0])
+            drain(dst.at[span(g, q_far, 1)], give_r.at[ph, g, 2, 1])
 
         def settle(g):
-            for i in range(12):
-                drain(cut(src, g), ar_s.at[ph, g, i])
-
-        return open_, middle, own, pass_on, close, settle
+            for i in range(6):
+                drain(dst.at[0:half], give_s.at[ph, g, i])
+
+        return offer, pass_on, close, settle
 
     def small_steps(g, step):
-        size = math.gcd(64, ne * unit)
-        base, length = lanes[g]
-        first = base // size
-        lax.fori_loop(first, first + ne * length // size, lambda m, c: (step(at(m, size)), c)[1], 0)
+        size = math.gcd(64, lane)
+        lax.fori_loop(g * (lane // size), (g + 1) * (lane // size), lambda m, c: (step(at(m, size)), c)[1], 0)
 
     def round_into(src, columns, g):
         def some(there):
@@ -277,7 +257,7 @@
         ret_in[st, k, rows_of(g, e), :] = ret_out[k, rows_of(g, e), :]
 
     def settle_ret(ph, g):
-        loop(nk, lambda k: drain(ret_out.at[k, 0 : (ne - 1) * lanes[g][1]], rx_s.at[ph, k, g]))
+        loop(nk, lambda k: drain(ret_out.at[k, 0 : (ne - 1) * unit], rx_s.at[ph, k, g]))
 
     def settle_yret(ph):
         loop(nk, lambda k: drain(yret_out.at[k, 0 : (nd - 1) * rows], ry_s.at[ph, k]))
@@ -285,8 +265,8 @@
     short = nd * rows // 2
 
     def collect(ph, st, t, k):
-        for g in range(2):
-            drain(ret_in.at[st, k, 0 : (ne - 1) * lanes[g][1]], rx_r.at[ph, k, g])
+        for g in lanes:
+            drain(ret_in.at[st, k, 0 : (ne - 1) * unit], rx_r.at[ph, k, g])
 
         def some(m):
             yret_out[k, at(m, short), :] = jnp.dot(
@@ -310,12 +290,14 @@
 
         small_steps(g, some)
 
-    def forward_down(ph, g):
+    def forward_down(ph, g, beside=None):
         mine = span_of(g)
 
         def down(k):
             ret_out[k, mine, :] = jnp.dot(act[mine, :], wdc[k], preferred_element_type=F32).astype(BF16)
             ret_send(ph, 0, g, k)
+            if beside is not None:
+                beside(k)
 
         loop(nk, down)
 
@@ -324,17 +306,18 @@
         for m in range(total // wide):
             act_t[t, :, m * wide : (m + 1) * wide] = act[m * wide : (m + 1) * wide, :].T
 
-    def before(t, g, with_act):
+    def pre_grads(gate, up, grad):
+        s = jax.nn.sigmoid(gate)
+        silu = gate * s
+        return grad * up * s * (1.0 + gate * (1.0 - s)), grad * silu, silu * up
+
+    def before(t, g):
         def some(there):
             gate = gate_up[t, there, 0:hidden].astype(F32)
             up = gate_up[t, there, hidden : 2 * hidden].astype(F32)
-            grad = grad_act[there, :].astype(F32)
-            s = jax.nn.sigmoid(gate)
-            silu = gate * s
-            if with_act:
-                act[there, :] = (silu * up).astype(BF16)
-            gate_up[t, there, 0:hidden] = (grad * up * s * (1.0 + gate * (1.0 - s))).astype(BF16)
-            gate_up[t, there, hidden : 2 * hidden] = (grad * silu).astype(BF16)
+            of_gate, of_up, _ = pre_grads(gate, up, grad_act[there, :].astype(F32))
+            gate_up[t, there, 0:hidden] = of_gate.astype(BF16)
+            gate_up[t, there, hidden : 2 * hidden] = of_up.astype(BF16)
 
         small_steps(g, some)
 
@@ -396,41 +379,49 @@
         wdc[k] = down.astype(BF16)
         pltpu.make_async_copy(wdc.at[k], gd.at[:, at(k, kc)], store_sem.at[3]).start()
 
-    lag = 2
-
     def when(test, step):
         @pl.when(test)
         def _():
             step()
 
-    def forward_to_sums(ph, st, t, sums):
-        open_, middle, own, pass_on, close, settle = sums
+    lag = 2
+
+    def forward_to_sums(ph, st, t, sums, mine, gives):
+        open_, middle = sums[0], sums[1]
         acc[...] = jnp.zeros_like(acc)
 
         def step(i):
-            def first():
-                y_wait(ph, st, i)
-                x_send(ph, st, t, i, 0)
-
-            when(i < nk, first)
-            when(i >= lag, lambda: x_send(ph, st, t, i - lag, 1))
-            when(i >= 1, lambda: forward_chunk(ph, i - 1, 0))
-            when(i >= lag + 1, lambda: forward_chunk(ph, i - lag - 1, 1))
-
-        loop(nk + 1, step)
-        round_into(rs_f, 2 * hidden, 0)
-        open_(0)
-        for k in range(nk + 1 - lag, nk):
-            x_send(ph, st, t, k, 1)
-        for n, k in enumerate(range(nk - lag, nk)):
-            forward_chunk(ph, k, 1)
-            if n == 0:
-                middle(0)
-        own(0)
-        round_into(rs_f, 2 * hidden, 1)
-        open_(1)
-        pass_on(0)
+            for g in lanes:
+                def first(g=g):
+                    if g == 0:
+                        y_wait(ph, st, i)
+                    x_send(ph, st, t, i - g * lag, g)
+
+                when((i >= g * lag) & (i < nk + g * lag), first)
+            for g in lanes:
+                when((i >= g * lag + 1) & (i < nk + g * lag + 1), lambda g=g: forward_chunk(ph, i - g * lag - 1, g))
+
+        def start(g):
+            round_into(rs_f, 2 * hidden, g)
+            open_(g)
+
+        def run(first, last):
+            lax.fori_loop(first, last, lambda i, c: (step(i), c)[1], 0)
+
+        run(0, nk + 1)
+        start(0)
+        run(nk + 1, nk + 2)
+        middle(0)
+        run(nk + 2, nk + 3)
+        start(1)
+        mine(0)
+        run(nk + 3, nk + 4)
+        gives[1](0)
         middle(1)
+        run(nk + 4, nk + 5)
+        start(2)
+        mine(1)
+        middle(2)
 
     gain_acc[...] = jnp.zeros_like(gain_acc)
     loop(nk, lambda k: y_send(0, 0, norm, k))
@@ -439,90 +430,96 @@
     drain(wdc, load_sem.at[2])
     drain(cotc, load_sem.at[3])
 
-    sums = all_sum(0, rs_f, gate_up.at[0], one_f, two_f, 2 * hidden)
-    forward_to_sums(0, 0, 0, sums)
-    sums[4](0)
+    sums = summing(0, rs_f, one_f, two_f)
+    gives = giving(0, gate_up.at[0])
+
+    def mine0(g):
+        for h in range(2):
+            gate_up[0, span(g, q, h), :] = sums[2](g, h).astype(BF16)
+        gives[0](g)
+
+    forward_to_sums(0, 0, 0, sums, mine0, gives)
+    gives[2](0)
     activate(0, 0)
     forward_down(0, 0)
-    sums[2](1)
-    sums[3](1)
+    gives[1](1)
+    mine0(2)
     settle_y(0, 0)
     settle_x(0)
-    sums[4](1)
+    gives[2](1)
     activate(0, 1)
     forward_down(0, 1)
+    gives[1](2)
     acc[:, 0:hidden] = jnp.zeros((total, hidden), F32)
+    gives[2](2)
+    activate(0, 2)
+    forward_down(0, 2, lambda k: y_send(2, 1, cotc, k))
 
     def turn_round(i):
-        def first():
-            collect(0, 0, 0, i)
-            y_send(2, 1, cotc, i)
-
         def second():
             k = i - 1
             add_rows(0, tokc, k)
             send(yret_in.at[0, k], hid1.at[k], z_s.at[0, k], z_r.at[0, k], pipe=p_up)
             y_wait(2, 1, k)
-            x_send(2, 1, 1, k, 0)
-            x_send(2, 1, 1, k, 1)
-
-        def third():
-            backward_chunk(2, i - 2, 0)
-            backward_chunk(2, i - 2, 1)
-
-        when(i < nk, first)
+            for g in lanes:
+                x_send(2, 1, 1, k, g)
+
+        when(i < nk, lambda: collect(0, 0, 0, i))
         when((i >= 1) & (i <= nk), second)
-        when(i >= 2, third)
+        when(i >= 2, lambda: backward_chunk(2, i - 2))
 
     loop(nk + 2, turn_round)
-    sums[5](0)
-    sums[5](1)
-    sums_b = all_sum(2, rs_b, grad_act, one_b, two_b, hidden)
-    for g in range(2):
+    sums_b = summing(2, rs_b, one_b, two_b)
+    for g in lanes:
         round_into(rs_b, hidden, g)
         sums_b[0](g)
     turn(0)
-    settle_ret(0, 0)
-    settle_ret(0, 1)
+    for g in lanes:
+        sums[3](g)
+        gives[3](g)
+        settle_ret(0, g)
     settle_yret(0)
     settle_y(2, 1)
     settle_x(2)
-    for g in range(2):
-        sums_b[1](g)
 
     def arrived(k, c):
         drain(hid1.at[k], z_r.at[0, k])
         return squares(hid1, k, c)
 
     so_far = lax.fori_loop(0, nk - 1, arrived, none)
-    for g in range(2):
-        sums_b[2](g)
+    for g in lanes:
+        sums_b[1](g)
     normalize(1, hid1, arrived(nk - 1, so_far))
     loop(nk, lambda k: drain(yret_in.at[0, k], z_s.at[0, k]))
 
     loop(nk, lambda k: y_send(1, 0, norm, k))
-    for g in range(2):
-        sums_b[3](g)
-    for g in range(2):
-        sums_b[4](g)
-    sums = all_sum(1, rs_f, gate_up.at[1], one_f, two_f, 2 * hidden)
-    forward_to_sums(1, 0, 1, sums)
-
-    sums[4](0)
-    sums[5](0)
-    before(1, 0, True)
+    sums = summing(1, rs_f, one_f, two_f)
+    gives = giving(1, gate_up.at[1])
+
+    def mine1(g):
+        for h in range(2):
+            there = span(g, q, h)
+            both = sums[2](g, h)
+            of_gate, of_up, activated = pre_grads(both[:, 0:hidden], both[:, hidden : 2 * hidden], sums_b[2](g, h))
+            gate_up[1, there, 0:hidden] = of_gate.astype(BF16)
+            gate_up[1, there, hidden : 2 * hidden] = of_up.astype(BF16)
+            act[there, :] = activated.astype(BF16)
+        gives[0](g)
+
+    forward_to_sums(1, 0, 1, sums, mine1, gives)
+
+    gives[2](0)
     backward_up(2, 1, 0)
-    sums[2](1)
-    sums[3](1)
+    gives[1](1)
+    mine1(2)
     settle_y(1, 0)
     settle_x(1)
-    sums_b[5](0)
-    sums_b[5](1)
-    sums[4](1)
-    sums[5](1)
-    before(1, 1, True)
+    gives[2](1)
     backward_up(2, 1, 1)
+    gives[1](2)
     mean_acc[...] = jnp.zeros_like(mean_acc)
+    gives[2](2)
+    backward_up(2, 1, 2)
 
     def back1(i):
         when(i < nk, lambda: collect(2, 1, 1, i))
@@ -536,11 +533,16 @@
         send(yret_in.at[1, k], grad0.at[k], z_s.at[1, k], z_r.at[1, k], pipe=p_down)
 
     loop(nk, leave)
-    settle_ret(2, 0)
-    settle_ret(2, 1)
+
+    acts = giving(4, act)
+    for g in lanes:
+        acts[0](g)
+    for g in lanes:
+        sums[3](g)
+        gives[3](g)
+        sums_b[3](g)
+        settle_ret(2, g)
     settle_yret(2)
-
-    forward_down(1, 0)
     acc[:, 0:hidden] = jnp.zeros((total, hidden), F32)
 
     def come(i):
@@ -550,41 +552,49 @@
 
         def second():
             y_wait(3, 1, i - 1)
-            x_send(3, 1, 0, i - 1, 0)
-            x_send(3, 1, 0, i - 1, 1)
-
-        def third():
-            backward_chunk(3, i - 2, 0)
-            backward_chunk(3, i - 2, 1)
+            for g in lanes:
+                x_send(3, 1, 0, i - 1, g)
 
         when(i < nk, first)
         when((i >= 1) & (i <= nk), second)
-        when(i >= 2, third)
-
-    loop(nk + 2, come)
+        when(i >= 2, lambda: backward_chunk(3, i - 2))
+
+    loop(1, come)
+    for g in lanes:
+        acts[1](g)
+    for g in lanes:
+        acts[2](g)
+    forward_down(1, 0)
+    turn(1)
+    lax.fori_loop(1, nk + 2, lambda i, c: (come(i), c)[1], 0)
     loop(nk, lambda k: drain(yret_in.at[1, k], z_s.at[1, k]))
-    sums_b = all_sum(3, rs_b, grad_act, one_b, two_b, hidden)
-    for g in range(2):
+    sums_b = summing(3, rs_b, one_b, two_b)
+    gives = giving(3, grad_act)
+
+    def mine3(g):
+        for h in range(2):
+            grad_act[span(g, q, h), :] = sums_b[2](g, h).astype(BF16)
+        gives[0](g)
+
+    for g in lanes:
         round_into(rs_b, hidden, g)
         sums_b[0](g)
     forward_down(1, 1)
-    for g in range(2):
+    for g in lanes:
         sums_b[1](g)
-    sums_b[2](0)
-    sums_b[2](1)
-    turn(1)
-    sums_b[3](0)
-    sums_b[3](1)
-    settle_ret(1, 0)
-    sums_b[4](0)
-    before(0, 0, False)
-    backward_up(3, 0, 0)
-    settle_ret(1, 1)
-    sums_b[4](1)
-    before(0, 1, False)
-    backward_up(3, 0, 1)
+    forward_down(1, 2)
+    for g in lanes:
+        mine3(g)
+        if g >= 1:
+            gives[1](g - 1)
+    gives[1](CAP - 1)
     settle_y(3, 1)
     settle_x(3)
+    for g in lanes:
+        gives[2](g)
+        before(0, g)
+        settle_ret(1, g)
+        backward_up(3, 0, g)
 
     def leave1(i):
         when(i < nk, lambda: collect(1, 0, 1, i))
@@ -635,10 +645,11 @@
     drain(gain_all.at[0 : nd - 1], gain_r.at[2])
     gain_out[...] = jnp.broadcast_to(jnp.sum(gain_all[...], axis=2, keepdims=True), gain_out.shape)
 
-    sums_b[5](0)
-    sums_b[5](1)
-    settle_ret(3, 0)
-    settle_ret(3, 1)
+    for g in lanes:
+        sums_b[3](g)
+        gives[3](g)
+        acts[3](g)
+        settle_ret(3, g)
     settle_yret(3)
     drain(gain_dp.at[0 : nd - 1], gain_s.at[0])
     drain(gain_ex.at[0 : ne - 1], gain_s.at[1])
@@ -651,19 +662,26 @@
 
 
 def hand_over(quarter, kc, *refs):
-    got, given, sems = refs[0:6], refs[6:12], refs[12]
-    copies = []
-    for n, i in enumerate((3, 4, 5, 0, 1)):
-        size = got[i].shape[0] // 2
-        for h in range(2):
-            part = pl.ds(h * size, size)
-            copies.append(pltpu.make_async_copy(got[i].at[part], given[i].at[part], sems.at[n, h]))
-            copies[-1].start()
+    got, given, stages, sems = refs[0:6], refs[6:12], refs[12:17], refs[17]
+    order = (3, 4, 5, 0, 1)
+
+    def piece(n, h, way):
+        size = stages[n].shape[0] // 2
+        part = pl.ds(h * size, size)
+        ends = (got[order[n]].at[part], stages[n].at[part], given[order[n]].at[part])
+        return pltpu.make_async_copy(ends[way], ends[way + 1], sems.at[way, n, h])
+
+    each = [(n, h) for n in range(len(order)) for h in range(2)]
+    for n, h in each:
+        piece(n, h, 0).start()
     for j in range(got[2].shape[0]):
         for k in range(got[2].shape[1]):
             given[2][0:1, j * quarter + k * kc : j * quarter + (k + 1) * kc] = got[2][j, k, 0:1, :]
-    for copy in copies:
-        copy.wait()
+    for n, h in each:
+        piece(n, h, 0).wait()
+        piece(n, h, 1).start()
+    for n, h in each:
+        piece(n, h, 1).wait()
 
 
 def body(tokens, cotangent, gain, w_gate, w_up, w_down, route):
@@ -675,7 +693,7 @@
     nk = quarter // kc
     block = nd * CAP * TILE
     total = ne * block
-    half = (CAP - 1) * total // CAP // nd // 2
+    half = total // CAP // nd // 2
     table = route[0, :, :, 0]
     dest = []
     for t in range(PASSES):
@@ -724,10 +742,10 @@
             V((total, hidden), BF16),
             V((total, 2 * hidden), BF16),
             V((total, hidden), BF16),
-            V((2, 2, half, 2 * hidden), BF16),
-            V((2, 2, half, hidden), BF16),
-            V((2, 2, 2, half, 2 * hidden), BF16),
-            V((2, 2, 2, half, hidden), BF16),
+            V((CAP, 2, half, 2 * hidden), BF16),
+            V((CAP, 2, half, hidden), BF16),
+            V((CAP, 2, 2, half, 2 * hidden), BF16),
+            V((CAP, 2, 2, half, hidden), BF16),
             V((nk, total, kc), BF16),
             V((2, nk, total, kc), BF16),
             V((nk, nd * rows, kc), BF16),
@@ -744,18 +762,19 @@
             S(()),
             S((4, nk)),
             S((4, nk)),
-            S((4, nk, 2)),
-            S((4, nk, 2)),
-            S((4, nk, 2)),
-            S((4, nk, 2)),
+            S((4, nk, CAP)),
+            S((4, nk, CAP)),
+            S((4, nk, CAP)),
+            S((4, nk, CAP)),
             S((4, nk)),
             S((4, nk)),
             S((2, nk)),
             S((2, nk)),
-            S((4, 2, 12)),
-            S((4, 2, 2)),
-            S((4, 2, 2, 2)),
-            S((4, 2, 3, 2)),
+            S((4, CAP, 6)),
+            S((4, CAP, 2)),
+            S((4, CAP, 2, 2)),
+            S((5, CAP, 6)),
+            S((5, CAP, 3, 2)),
             S((3,)),
             S((3,)),
         ],
@@ -778,7 +797,8 @@
         ),
         in_specs=[hbm, hbm, vmem, hbm, hbm, hbm],
         out_specs=(hbm, hbm, vmem, hbm, hbm, hbm),
-        scratch_shapes=[S((5, 2))],
+        scratch_shapes=[V(results[i].shape, BF16) for i in (3, 4, 5, 0, 1)] + [S((2, 5, 2))],
+        compiler_params=pltpu.CompilerParams(vmem_limit_bytes=40_000_000),
     )(*results)
     return (
         out_rows[None],

time: 643 us -> 378 us (0.59)
  Pallas kernels: 640 us -> 367 us
  local copies, waits for them, and re-layouts: 0.77 us -> 8.94 us
    pallas_call x1, Pallas kernels: 261 us -> 6.78 us  [body(): pl.pallas_call(functools.partial(hand_over, quarter, kc), out_shape=(resu...]
    pallas_call x1, Pallas kernels: 380 us -> 360 us  [body(): pl.pallas_call(functools.partial(kernel, (nd, npipe, ne, rows, width, hid...]
    unnamed x0 -> x12, local copies, waits for them, and re-layouts: none -> 8.17 us
where the time goes in v3:
time: 378 us; the launch traced here: 377 us
  Pallas kernels  367 us (97%)
  local copies, waits for them, and re-layouts  8.94 us (2%)
    pallas_call x1, Pallas kernels, body(): pl.pallas_call(functools.partial(kernel, (nd, npipe, ne, rows, width, hid...  360 us
    unnamed x12, local copies, waits for them, and re-layouts  8.17 us

profile of v3, /device:TPU:1, one launch (start us, length us, event | category | flops | bytes accessed | tf_op | source)
XLA Modules:
  0.0 377.5 jit_solution(2559884652642671026)
XLA Ops:
  0.7 0.7 convert_bitcast_fusion.1
  1.4 0.1 broadcast_in_dim.25
  1.4 0.1 broadcast_in_dim.26
  1.5 0.6 broadcast_in_dim.27.dest
  2.1 360.2 %shard_map.118 = (bf16[128,5120]{1,0:T(8,128)(2,1)}, bf16[128,5120]{1,0:T(8,128)(2,1)}, f32[4,5,8,256]{3,2,1,0:T(8,128)}, bf16[1280,768]{1,0:T(8,128)(2,1)}, bf1...) custom-call(f32[2,8,128]{2,1,0:T(8,128)} %broadcast_in_dim.27.dest, bf16[128,5120]{1,0:T(8,128)(2,1)} %bitcast.20, ...), custom_call_target="tpu_custom_call" | custom-call | flops 27179089920 | bytes 17825792 | tf_op jit(solution)/shard_map/pallas_call | solution.py:711
  362.4 0.0 copy-start
  362.4 1.5 copy-done
  363.9 0.0 copy-start.1
  363.9 1.5 copy-done.1
  365.5 0.0 copy-start.2
  365.5 1.5 copy-done.2
  367.0 0.0 copy-start.3
  367.0 1.3 copy-done.3
  368.3 0.0 copy-start.4
  368.3 1.3 copy-done.4
  369.6 0.0 copy-start.5
  369.6 0.9 copy-done.5
  370.6 6.8 %shard_map.119 = (bf16[128,5120]{1,0:T(8,128)(2,1)}, bf16[128,5120]{1,0:T(8,128)(2,1)}, f32[1,5120]{1,0:T(1,128)}, bf16[1280,768]{1,0:T(8,128)(2,1)}, bf16[1280,...) custom-call(bf16[128,5120]{1,0:T(8,128)(2,1)S(1)} %copy-done.3, bf16[128,5120]{1,0:T(8,128)(2,1)S(1)} %copy-done.4, ...), custom_call_target="tpu_custom_call" | custom-call | tf_op jit(solution)/shard_map/pallas_call | solution.py:788
  (1 shorter events, 0.0 us)
Async XLA Ops:
  362.4 1.5 copy-start
  363.9 1.5 copy-start.1
  365.5 1.5 copy-start.2
  367.0 1.3 copy-start.3
  368.3 1.3 copy-start.4
  369.6 0.9 copy-start.5

commit v4 on v3

--- a/solution.py
+++ b/solution.py
@@ -24,9 +24,9 @@
     tokc, cotc, hid1, grad0, norm, wgu, wdc, dest_own, dest_all, place, back,
     yin, xout, xin, acc, gate_up, act, act_t, grad_act,
     rs_f, rs_b, one_f, one_b, two_f, two_b,
-    ret_out, ret_in, yret_out, yret_in, inverse, mean_acc, gain_acc, gain_dp, gain_ex, gain_all,
+    ret_out, ret_in, yret_out, yret_in, inverse, mean_acc, gain_acc, gain_dp, gain_ex, gain_all, way,
     load_sem, store_sem, dest_s, dest_r, y_s, y_r, x_s, x_r, rx_s, rx_r, ry_s, ry_r,
-    z_s, z_r, sum_s, one_r, two_r, give_s, give_r, gain_s, gain_r,
+    z_s, z_r, way_s, way_r, sum_s, one_r, two_r, give_s, give_r, gain_s, gain_r,
 ):
     nd, npipe, ne, rows, width, hidden = sizes
     quarter = width // nd
@@ -96,35 +96,34 @@
     def squares(ref, k, before):
         for j in range(nd):
             wide = ref[k, j].astype(F32)
-            before = before + jnp.sum(wide * wide, axis=-1, keepdims=True)
+            before = before + wide * wide
         return before
 
-    def normalize(t, ref, total_squares):
-        inverse[t] = lax.rsqrt(total_squares / width + epsilon)
-
-        def step(k):
-            for j in range(nd):
-                norm[k, j] = (ref[k, j].astype(F32) * inverse[t] * gain_of(k, j)).astype(BF16)
-
-        loop(nk, step)
-
-    none = jnp.zeros((rows, 1), F32)
-    normalize(0, tokc, lax.fori_loop(0, nk, lambda k, c: squares(tokc, k, c), none))
+    def scale(t, squared):
+        inverse[t] = lax.rsqrt(jnp.sum(squared, axis=-1, keepdims=True) / width + epsilon)
+
+    def normalize(t, ref, k):
+        for j in range(nd):
+            norm[k, j] = (ref[k, j].astype(F32) * inverse[t] * gain_of(k, j)).astype(BF16)
+
+    none = jnp.zeros((rows, kc), F32)
+    scale(0, lax.fori_loop(0, nk, lambda k, c: squares(tokc, k, c), none))
     pl.semaphore_wait(barrier, nd - 1 + ne - 1 + 2)
 
-    row_tile = lax.broadcasted_iota(jnp.int32, (rows, rows), 1) // TILE
-    row_at = lax.broadcasted_iota(jnp.int32, (1, rows), 1)
-    earlier = (row_tile.T < row_tile)
-    for t in range(PASSES):
-        expert_of = jnp.broadcast_to(dest[t, 0:1, :], (rows, rows))
-        same = jnp.where(earlier & (expert_of.T == expert_of), 1.0, 0.0).astype(F32)
-        rank = jnp.sum(same, axis=0, keepdims=True) / TILE
-        inner = (q * TILE + row_at % TILE).astype(F32)
-        mine = dest[t, 0:1, :]
-        dest_own[t] = jnp.broadcast_to(rank * lane + mine * unit + inner, (8, rows))
-    for d in range(1, nd):
-        send(dest_own, dest_all.at[q], dest_s, dest_r, dp=lax.rem(q + d, nd))
-    dest_all[q] = dest_own[...]
+    def work_out_places():
+        row_tile = lax.broadcasted_iota(jnp.int32, (rows, rows), 1) // TILE
+        row_at = lax.broadcasted_iota(jnp.int32, (1, rows), 1)
+        earlier = (row_tile.T < row_tile)
+        for t in range(PASSES):
+            expert_of = jnp.broadcast_to(dest[t, 0:1, :], (rows, rows))
+            same = jnp.where(earlier & (expert_of.T == expert_of), 1.0, 0.0).astype(F32)
+            rank = jnp.sum(same, axis=0, keepdims=True) / TILE
+            inner = (q * TILE + row_at % TILE).astype(F32)
+            mine = dest[t, 0:1, :]
+            dest_own[t] = jnp.broadcast_to(rank * lane + mine * unit + inner, (8, rows))
+        for d in range(1, nd):
+            send(dest_own, dest_all.at[q], dest_s, dest_r, dp=lax.rem(q + d, nd))
+        dest_all[q] = dest_own[...]
 
     def build_places():
         drain(dest_all.at[0 : nd - 1], dest_r)
@@ -263,6 +262,18 @@
         loop(nk, lambda k: drain(yret_out.at[k, 0 : (nd - 1) * rows], ry_s.at[ph, k]))
 
     short = nd * rows // 2
+
+    def collect_late(ph, st, t, k):
+        for g in lanes:
+            drain(ret_in.at[st, k, 0 : (ne - 1) * unit], rx_r.at[ph, k, g])
+        for j in range(nd):
+            norm[k, j] = jnp.dot(
+                back[t, j * rows : (j + 1) * rows, :], ret_in[st, k], preferred_element_type=F32
+            ).astype(BF16)
+        for d in range(1, nd):
+            j = lax.rem(q + d, nd)
+            send(norm.at[k, j], yret_in.at[st, k, q], ry_s.at[ph, k], ry_r.at[ph, k], dp=j)
+        yret_in[st, k, q] = norm[k, q]
 
     def collect(ph, st, t, k):
         for g in lanes:
@@ -379,6 +390,20 @@
         wdc[k] = down.astype(BF16)
         pltpu.make_async_copy(wdc.at[k], gd.at[:, at(k, kc)], store_sem.at[3]).start()
 
+    def long_way(d, src, dst, where):
+        def leave_():
+            send(src, way.at[d, 0], z_s.at[d, 0], way_r.at[d, 0], pipe=where)
+
+        def hop1():
+            drain(way.at[d, 0], way_r.at[d, 0])
+            send(way.at[d, 0], way.at[d, 1], way_s.at[d, 0], way_r.at[d, 1], pipe=where)
+
+        def hop2():
+            drain(way.at[d, 1], way_r.at[d, 1])
+            send(way.at[d, 1], dst, way_s.at[d, 1], z_r.at[d, 0], pipe=where)
+
+        return leave_, hop1, hop2
+
     def when(test, step):
         @pl.when(test)
         def _():
@@ -423,8 +448,13 @@
         mine(1)
         middle(2)
 
+    def norm_out0(k):
+        normalize(0, tokc, k)
+        y_send(0, 0, norm, k)
+
+    loop(nk, norm_out0)
+    work_out_places()
     gain_acc[...] = jnp.zeros_like(gain_acc)
-    loop(nk, lambda k: y_send(0, 0, norm, k))
     build_places()
     drain(wgu, load_sem.at[1])
     drain(wdc, load_sem.at[2])
@@ -455,11 +485,17 @@
     activate(0, 2)
     forward_down(0, 2, lambda k: y_send(2, 1, cotc, k))
 
+    round0 = long_way(0, yret_in.at[0, 0], hid1.at[0], p_down)
+
     def turn_round(i):
         def second():
             k = i - 1
             add_rows(0, tokc, k)
-            send(yret_in.at[0, k], hid1.at[k], z_s.at[0, k], z_r.at[0, k], pipe=p_up)
+            when(k == 0, round0[0])
+            when(
+                k > 0,
+                lambda: send(yret_in.at[0, k], hid1.at[k], z_s.at[0, k], z_r.at[0, k], pipe=p_up),
+            )
             y_wait(2, 1, k)
             for g in lanes:
                 x_send(2, 1, 1, k, g)
@@ -467,7 +503,10 @@
         when(i < nk, lambda: collect(0, 0, 0, i))
         when((i >= 1) & (i <= nk), second)
         when(i >= 2, lambda: backward_chunk(2, i - 2))
-
+        when(i == hop_at[0], round0[1])
+        when(i == hop_at[1], round0[2])
+
+    hop_at = (min(3, nk), min(5, nk + 1))
     loop(nk + 2, turn_round)
     sums_b = summing(2, rs_b, one_b, two_b)
     for g in lanes:
@@ -486,13 +525,17 @@
         drain(hid1.at[k], z_r.at[0, k])
         return squares(hid1, k, c)
 
-    so_far = lax.fori_loop(0, nk - 1, arrived, none)
+    so_far = lax.fori_loop(1, nk, arrived, none)
     for g in lanes:
         sums_b[1](g)
-    normalize(1, hid1, arrived(nk - 1, so_far))
+    scale(1, arrived(0, so_far))
     loop(nk, lambda k: drain(yret_in.at[0, k], z_s.at[0, k]))
 
-    loop(nk, lambda k: y_send(1, 0, norm, k))
+    def norm_out1(k):
+        normalize(1, hid1, k)
+        y_send(1, 0, norm, k)
+
+    loop(nk, norm_out1)
     sums = summing(1, rs_f, one_f, two_f)
     gives = giving(1, gate_up.at[1])
 
@@ -528,9 +571,15 @@
     loop(nk + 1, back1)
     mean = mean_of()
 
+    round1 = long_way(1, yret_in.at[1, 0], grad0.at[0], p_up)
+
     def leave(k):
         finish_grads(1, hid1, cotc, k, mean)
-        send(yret_in.at[1, k], grad0.at[k], z_s.at[1, k], z_r.at[1, k], pipe=p_down)
+        when(k == 0, round1[0])
+        when(
+            k > 0,
+            lambda: send(yret_in.at[1, k], grad0.at[k], z_s.at[1, k], z_r.at[1, k], pipe=p_down),
+        )
 
     loop(nk, leave)
 
@@ -547,19 +596,23 @@
 
     def come(i):
         def first():
-            drain(grad0.at[i], z_r.at[1, i])
-            y_send(3, 1, grad0, i)
+            k = lax.rem(i + 1, nk)
+            drain(grad0.at[k], z_r.at[1, k])
+            y_send(3, 1, grad0, k)
 
         def second():
-            y_wait(3, 1, i - 1)
+            k = lax.rem(i, nk)
+            y_wait(3, 1, k)
             for g in lanes:
-                x_send(3, 1, 0, i - 1, g)
+                x_send(3, 1, 0, k, g)
 
         when(i < nk, first)
         when((i >= 1) & (i <= nk), second)
-        when(i >= 2, lambda: backward_chunk(3, i - 2))
+        when(i >= 2, lambda: backward_chunk(3, lax.rem(i - 1, nk)))
+        when(i == 1, round1[2])
 
     loop(1, come)
+    round1[1]()
     for g in lanes:
         acts[1](g)
     for g in lanes:
@@ -596,17 +649,8 @@
         settle_ret(1, g)
         backward_up(3, 0, g)
 
-    def leave1(i):
-        when(i < nk, lambda: collect(1, 0, 1, i))
-
-        def second():
-            add_rows(1, hid1, i - 1)
-            to_rows(yret_in.at[0], i - 1, out_tok, store_sem.at[0])
-
-        when(i >= 1, second)
-
-    loop(nk + 1, leave1)
-    settle_yret(1)
+    early = min(2, nk)
+    loop(early, lambda k: collect_late(1, 0, 1, k))
     mean_acc[...] = jnp.zeros_like(mean_acc)
 
     def back0(i):
@@ -618,6 +662,7 @@
     for d in range(1, nd):
         j = lax.rem(q + d, nd)
         send(gain_acc.at[j], gain_dp.at[q], gain_s.at[0], gain_r.at[0], dp=j)
+    lax.fori_loop(early, nk, lambda k, c: (collect_late(1, 0, 1, k), c)[1], 0)
     mean = mean_of()
 
     def last(k):
@@ -635,6 +680,12 @@
     for d in range(1, ne):
         send(gain_ex.at[e], gain_ex.at[e], gain_s.at[1], gain_r.at[1], expert=lax.rem(e + d, ne))
     weight_grads(nk - 1)
+
+    def leave1(k):
+        add_rows(1, hid1, k)
+        to_rows(yret_in.at[0], k, out_tok, store_sem.at[0])
+
+    loop(nk, leave1)
     drain(gain_ex.at[0 : ne - 1], gain_r.at[1])
     mine = gain_ex[0]
     for j in range(1, ne):
@@ -651,6 +702,10 @@
         acts[3](g)
         settle_ret(3, g)
     settle_yret(3)
+    loop(nk, lambda k: drain(norm.at[k, 0 : nd - 1], ry_s.at[1, k]))
+    for d in range(2):
+        for i in range(2):
+            drain(way.at[d, i], way_s.at[d, i])
     drain(gain_dp.at[0 : nd - 1], gain_s.at[0])
     drain(gain_ex.at[0 : ne - 1], gain_s.at[1])
     drain(gain_all.at[0 : nd - 1], gain_s.at[2])
@@ -756,6 +811,7 @@
             V((nd, nk, 8, kc), F32),
             V((ne, nk, 8, kc), F32),
             V((nd, nk, 8, kc), F32),
+            V((2, 2) + chunks[1:], BF16),
             S((4,)),
             S((4,)),
             S(()),
@@ -770,6 +826,8 @@
             S((4, nk)),
             S((2, nk)),
             S((2, nk)),
+            S((2, 2)),
+            S((2, 2)),
             S((4, CAP, 6)),
             S((4, CAP, 2)),
             S((4, CAP, 2, 2)),

time: 378 us -> 383 us (1.013)
  Pallas kernels: 367 us -> 372 us
    pallas_call x1, Pallas kernels: 360 us -> 366 us  [body(): pl.pallas_call(functools.partial(kernel, (nd, npipe, ne, rows, width, hid...]
where the time goes in v4:
time: 383 us
  Pallas kernels  372 us (97%)
  local copies, waits for them, and re-layouts  8.94 us (2%)
    pallas_call x1, Pallas kernels, body(): pl.pallas_call(functools.partial(kernel, (nd, npipe, ne, rows, width, hid...  366 us
    unnamed x12, local copies, waits for them, and re-layouts  8.17 us

profile of v4, /device:TPU:1, one launch (start us, length us, event | category | flops | bytes accessed | tf_op | source)
XLA Modules:
  0.0 382.8 jit_solution(13206855309058146607)
XLA Ops:
  0.7 0.7 convert_bitcast_fusion.1
  1.4 0.1 broadcast_in_dim.25
  1.4 0.1 broadcast_in_dim.26
  1.5 0.6 broadcast_in_dim.27.dest
  2.1 365.5 %shard_map.118 = (bf16[128,5120]{1,0:T(8,128)(2,1)}, bf16[128,5120]{1,0:T(8,128)(2,1)}, f32[4,5,8,256]{3,2,1,0:T(8,128)}, bf16[1280,768]{1,0:T(8,128)(2,1)}, bf1...) custom-call(f32[2,8,128]{2,1,0:T(8,128)} %broadcast_in_dim.27.dest, bf16[128,5120]{1,0:T(8,128)(2,1)} %bitcast.20, ...), custom_call_target="tpu_custom_call" | custom-call | flops 27179089920 | bytes 17825792 | tf_op jit(solution)/shard_map/pallas_call | solution.py:766
  367.7 0.0 copy-start
  367.7 1.5 copy-done
  369.2 0.0 copy-start.1
  369.2 1.5 copy-done.1
  370.7 0.0 copy-start.2
  370.7 1.5 copy-done.2
  372.3 0.0 copy-start.3
  372.3 1.3 copy-done.3
  373.6 0.0 copy-start.4
  373.6 1.3 copy-done.4
  374.9 0.0 copy-start.5
  374.9 0.9 copy-done.5
  375.8 6.8 %shard_map.119 = (bf16[128,5120]{1,0:T(8,128)(2,1)}, bf16[128,5120]{1,0:T(8,128)(2,1)}, f32[1,5120]{1,0:T(1,128)}, bf16[1280,768]{1,0:T(8,128)(2,1)}, bf16[1280,...) custom-call(bf16[128,5120]{1,0:T(8,128)(2,1)S(1)} %copy-done.3, bf16[128,5120]{1,0:T(8,128)(2,1)S(1)} %copy-done.4, ...), custom_call_target="tpu_custom_call" | custom-call | tf_op jit(solution)/shard_map/pallas_call | solution.py:846
  (1 shorter events, 0.0 us)
Async XLA Ops:
  367.7 1.5 copy-start
  369.2 1.5 copy-start.1
  370.7 1.5 copy-start.2
  372.3 1.3 copy-start.3
  373.6 1.3 copy-start.4
  374.9 0.9 copy-start.5

commit v5 on v4

--- a/solution.py
+++ b/solution.py
@@ -301,14 +301,12 @@
 
         small_steps(g, some)
 
-    def forward_down(ph, g, beside=None):
+    def forward_down(ph, g):
         mine = span_of(g)
 
         def down(k):
             ret_out[k, mine, :] = jnp.dot(act[mine, :], wdc[k], preferred_element_type=F32).astype(BF16)
             ret_send(ph, 0, g, k)
-            if beside is not None:
-                beside(k)
 
         loop(nk, down)
 
@@ -452,8 +450,8 @@
         normalize(0, tokc, k)
         y_send(0, 0, norm, k)
 
+    work_out_places()
     loop(nk, norm_out0)
-    work_out_places()
     gain_acc[...] = jnp.zeros_like(gain_acc)
     build_places()
     drain(wgu, load_sem.at[1])
@@ -483,7 +481,7 @@
     acc[:, 0:hidden] = jnp.zeros((total, hidden), F32)
     gives[2](2)
     activate(0, 2)
-    forward_down(0, 2, lambda k: y_send(2, 1, cotc, k))
+    forward_down(0, 2)
 
     round0 = long_way(0, yret_in.at[0, 0], hid1.at[0], p_down)
 
@@ -500,7 +498,11 @@
             for g in lanes:
                 x_send(2, 1, 1, k, g)
 
-        when(i < nk, lambda: collect(0, 0, 0, i))
+        def first():
+            collect(0, 0, 0, i)
+            y_send(2, 1, cotc, i)
+
+        when(i < nk, first)
         when((i >= 1) & (i <= nk), second)
         when(i >= 2, lambda: backward_chunk(2, i - 2))
         when(i == hop_at[0], round0[1])
@@ -617,8 +619,6 @@
         acts[1](g)
     for g in lanes:
         acts[2](g)
-    forward_down(1, 0)
-    turn(1)
     lax.fori_loop(1, nk + 2, lambda i, c: (come(i), c)[1], 0)
     loop(nk, lambda k: drain(yret_in.at[1, k], z_s.at[1, k]))
     sums_b = summing(3, rs_b, one_b, two_b)
@@ -632,6 +632,7 @@
     for g in lanes:
         round_into(rs_b, hidden, g)
         sums_b[0](g)
+    forward_down(1, 0)
     forward_down(1, 1)
     for g in lanes:
         sums_b[1](g)
@@ -648,6 +649,8 @@
         before(0, g)
         settle_ret(1, g)
         backward_up(3, 0, g)
+
+    turn(1)
 
     early = min(2, nk)
     loop(early, lambda k: collect_late(1, 0, 1, k))

time: 383 us -> 367 us (0.958)
  Pallas kernels: 372 us -> 356 us
    pallas_call x1, Pallas kernels: 366 us -> 349 us  [body(): pl.pallas_call(functools.partial(kernel, (nd, npipe, ne, rows, width, hid...]
where the time goes in v5:
time: 367 us; the launch traced here: 366 us
  Pallas kernels  356 us (97%)
  local copies, waits for them, and re-layouts  8.94 us (2%)
    pallas_call x1, Pallas kernels, body(): pl.pallas_call(functools.partial(kernel, (nd, npipe, ne, rows, width, hid...  349 us
    unnamed x12, local copies, waits for them, and re-layouts  8.17 us

profile of v5, /device:TPU:1, one launch (start us, length us, event | category | flops | bytes accessed | tf_op | source)
XLA Modules:
  0.0 366.2 jit_solution(11680850015719415335)
XLA Ops:
  0.7 0.7 convert_bitcast_fusion.1
  1.4 0.1 broadcast_in_dim.25
  1.4 0.1 broadcast_in_dim.26
  1.5 0.6 broadcast_in_dim.27.dest
  2.1 349.0 %shard_map.118 = (bf16[128,5120]{1,0:T(8,128)(2,1)}, bf16[128,5120]{1,0:T(8,128)(2,1)}, f32[4,5,8,256]{3,2,1,0:T(8,128)}, bf16[1280,768]{1,0:T(8,128)(2,1)}, bf1...) custom-call(f32[2,8,128]{2,1,0:T(8,128)} %broadcast_in_dim.27.dest, bf16[128,5120]{1,0:T(8,128)(2,1)} %bitcast.20, ...), custom_call_target="tpu_custom_call" | custom-call | flops 27179089920 | bytes 17825792 | tf_op jit(solution)/shard_map/pallas_call | solution.py:769
  351.1 0.0 copy-start
  351.1 1.5 copy-done
  352.6 0.0 copy-start.1
  352.6 1.5 copy-done.1
  354.2 0.0 copy-start.2
  354.2 1.5 copy-done.2
  355.7 0.0 copy-start.3
  355.7 1.3 copy-done.3
  357.1 0.0 copy-start.4
  357.1 1.3 copy-done.4
  358.4 0.0 copy-start.5
  358.4 0.9 copy-done.5
  359.3 6.8 %shard_map.119 = (bf16[128,5120]{1,0:T(8,128)(2,1)}, bf16[128,5120]{1,0:T(8,128)(2,1)}, f32[1,5120]{1,0:T(1,128)}, bf16[1280,768]{1,0:T(8,128)(2,1)}, bf16[1280,...) custom-call(bf16[128,5120]{1,0:T(8,128)(2,1)S(1)} %copy-done.3, bf16[128,5120]{1,0:T(8,128)(2,1)S(1)} %copy-done.4, ...), custom_call_target="tpu_custom_call" | custom-call | tf_op jit(solution)/shard_map/pallas_call | solution.py:849
  (1 shorter events, 0.0 us)
Async XLA Ops:
  351.1 1.5 copy-start
  352.6 1.5 copy-start.1
  354.2 1.5 copy-start.2
  355.7 1.3 copy-start.3
  357.1 1.3 copy-start.4
  358.4 0.9 copy-start.5
